TPU v7x, 128 devices: a whole 4x4x4 slice. The times are simulated.
128 devices in a mesh: pair: 16 (over x_hi, y, core), aux: 8 (over x_lo, z).
Axes of the slice: x: 4 (x_hi: 2, x_lo: 2; x = x_hi * 2 + x_lo), y: 4, z: 4, core: 2. Of those that a mesh axis runs over, the one named last changes fastest.
Arguments:
- slab: bfloat16 [180224, 8192], P('pair', 'aux')
- density: bfloat16 [512, 64, 128], P(('pair', 'aux')), may hold values from -6 to 6
- block_list: int32 [1408], P('pair'), may hold values from 0 to 511
- block_sizes: int32 [1408], P('pair'), may hold values from 32 to 128, as said below
- metric: float32 [8192, 384], P('aux'), as said below
Outputs:
- coulomb: bfloat16 [1408, 64, 128], P(('pair', 'aux'))
- coeffs: float32 [64, 8192], P(None, 'aux')
Inputs may be any that keep to these rules, and one draw needn't show every extreme that they name: `block_sizes`: in each pair group's 88 slots at least one slot has 128 live pair functions. `metric`: each row's entry at column 128 + (row mod 128) exceeds the sum of the magnitudes of the row's other entries.
All inputs are finite; a program needn't handle non-finite values.
Results may differ from a plain program's by a relative error of at most 0.0042.
Values may be sent and summed in bfloat16 or wider, within the bound.
A program may use at most 128 MiB of HBM per device.

v0:
```python
import jax
import jax.numpy as jnp
from jax import lax
from jax.sharding import PartitionSpec as P

BS = 128
HB = 128
ITERS = 4


def padded_2(array, sides, width):
    for axis, dim in sides:
        size, length = (lax.axis_size(axis), array.shape[dim])
        up = [(i, (i + 1) % size) for i in range(size - 1)]
        down = [(j, i) for i, j in up]
        last = lax.slice_in_dim(array, length - width, length, axis=dim)
        first = lax.slice_in_dim(array, 0, width, axis=dim)
        before = lax.ppermute(last, axis, up)
        after = lax.ppermute(first, axis, down)
        array = jnp.concatenate([before, array, after], axis=dim)
    return array


def band_apply(metric, values_in):
    count_aux = values_in.shape[1]
    padded = padded_2(values_in, (("aux", 1),), HB)
    windows = jnp.stack(
        [
            padded[:, block_index * HB : block_index * HB + 3 * HB]
            for block_index in range(count_aux // HB)
        ]
    )
    blocks = metric.reshape(count_aux // HB, HB, 3 * HB)
    result = jnp.einsum("bpc,bdc->dbp", blocks, windows, precision=lax.Precision.HIGHEST)
    return result.reshape(values_in.shape[0], count_aux)


def jacobi_solve(fit_total, metric):
    row_index = jnp.arange(metric.shape[0], dtype=jnp.int32)
    diagonal = jnp.take_along_axis(metric, (HB + row_index % HB)[:, None], axis=1)[:, 0]
    coeffs = fit_total / diagonal
    for sweep in range(ITERS):
        coeffs = coeffs + (fit_total - band_apply(metric, coeffs)) / diagonal
    return coeffs


def shards(slab, density, block_list, block_sizes, metric):
    slot_count = block_list.shape[0]
    aux_local = slab.shape[1]
    tensor = slab.reshape(slot_count, BS, aux_local)
    shard_piece = lax.all_gather(density, ("pair", "aux"), axis=0, tiled=True)
    block_ids = jnp.arange(shard_piece.shape[0], dtype=jnp.int32)
    select = (block_list[:, None] == block_ids[None, :]).astype(jnp.bfloat16)
    gathered = jnp.einsum("sm,mdk->sdk", select, shard_piece, preferred_element_type=jnp.float32)
    live_rows = jnp.arange(BS, dtype=jnp.int32)[None, :] < block_sizes[:, None]
    picked = jnp.where(live_rows[:, None, :], gathered, 0.0).astype(jnp.bfloat16)
    partial_fit = jnp.einsum("sdk,skp->dp", picked, tensor, preferred_element_type=jnp.float32)
    fit_total = lax.psum(partial_fit, "pair")
    coeffs = jacobi_solve(fit_total, metric)
    coeff_b = coeffs.astype(jnp.bfloat16)
    own_slots = slot_count // lax.axis_size("aux")
    coulomb_mine = lax.psum_scatter(
        jnp.einsum("dp,skp->sdk", coeff_b, tensor, preferred_element_type=jnp.float32),
        "aux",
        scatter_dimension=0,
        tiled=True,
    )
    sizes_mine = lax.dynamic_slice_in_dim(block_sizes, lax.axis_index("aux") * own_slots, own_slots)
    live_mine = jnp.arange(BS, dtype=jnp.int32)[None, :] < sizes_mine[:, None]
    coulomb = jnp.where(live_mine[:, None, :], coulomb_mine, 0.0).astype(jnp.bfloat16)
    return (coulomb, coeffs)


def solution(mesh):
    return jax.shard_map(
        shards,
        mesh=mesh,
        in_specs=(
            P("pair", "aux"),
            P(("pair", "aux"), None, None),
            P("pair"),
            P("pair"),
            P("aux", None),
        ),
        out_specs=(P(("pair", "aux"), None, None), P(None, "aux")),
        check_vma=False,
    )
```

profile of v0, /device:TPU:0, one launch (start us, length us, event | category | flops | bytes accessed | tf_op | source)
XLA Modules:
  0.0 597.7 jit_solution(6880266263682452287)
XLA Ops:
  7.2 0.0 copy-start
  7.2 0.0 all-gather.2.cloned.1.call-start
  7.2 0.7 all-gather.2.cloned.1.call-update
  7.9 0.0 all-reduce.2.cloned.1.call-start
  8.0 0.7 iota_compare_fusion.1
  8.7 314.8 %all-gather.2.cloned.1.call-done = bf16[512,64,128]{2,1,0:T(8,128)(2,1)} async-done(((bf16[4,64,128]{2,1,0:T(8,128)(2,1)}), bf16[512,64,128]{2,1,0:T(8,128)(2,1)}) %all-gather.2.cloned.1.call-update) | async-done | bytes 8388624 | tf_op jit(solution)/shard_map/all_gather | solution.py:51
  323.5 8.5 %select_convert_fusion = bf16[88,64,128]{2,0,1:T(8,128)(2,1)S(1)} fusion(bf16[512,64,128]{2,1,0:T(8,128)(2,1)} %all-gather.2.cloned.1.call-done, pred[88,128]{1,0:T(8,128)(4,1)S(1)} %iota_compare_fusion.1, s32[88]{0:T(128)} %param.7), kind=kOutput, calls=%fused_computation.3 | convolution fusion | flops 739684352 | bytes 9842016 | tf_op jit(solution)/shard_map/sm,mdk->sdk/dot_general | solution.py:54
  332.0 10.4 %fusion.6 = f32[64,1024]{1,0:T(8,128)} fusion(bf16[88,128,1024]{2,1,0:T(8,128)(2,1)} %bitcast.195, bf16[88,64,128]{2,0,1:T(8,128)(2,1)S(1)} %select_convert_fusion), kind=kOutput, calls=%fused_computation.11 | convolution fusion | flops 1476395008 | bytes 24772608 | tf_op jit(solution)/shard_map/sdk,skp->dp/dot_general | solution.py:57
  342.4 0.0 all-reduce.2.cloned.1.call-update
  342.5 0.0 reduce-scatter.2.cloned.1.call-start
  342.5 0.0 copy-done
  342.5 8.6 %gather_fusion = f32[1024]{0:T(1024)S(1)} fusion(f32[1024,384]{1,0:T(8,128)S(1)} %copy-done, s32[1024]{0:T(1024)S(1)} %bitcast.197), kind=kCustom, calls=%fused_computation | custom fusion | bytes 16384 | tf_op jit(solution)/shard_map/jit(take_along_axis)/gather | solution.py:40
  351.2 130.0 %all-reduce.2.cloned.1.call-done = f32[64,1024]{1,0:T(8,128)} async-done(((f32[64,1024]{1,0:T(8,128)}), f32[64,1024]{1,0:T(8,128)}) %all-reduce.2.cloned.1.call-update) | async-done | bytes 262160 | tf_op jit(solution)/shard_map/psum | solution.py:58
  481.2 1.0 broadcast_divide_fusion
  482.2 3.5 collective-permute-start
  485.7 1.3 collective-permute-start.1
  487.0 0.3 collective-permute-done
  487.3 0.0 copy-start.1
  487.4 4.1 collective-permute-done.1
  491.5 2.3 convolution_bitcast_fusion.4
  493.8 0.0 copy-done.1
  493.8 3.5 collective-permute-start.2
  497.3 1.3 collective-permute-start.3
  498.6 0.3 collective-permute-done.2
  499.0 4.1 collective-permute-done.3
  503.1 2.3 convolution_bitcast_fusion.3
  505.4 0.1 fusion.14
  505.5 4.1 collective-permute-start.4
  509.6 1.5 collective-permute-start.5
  511.1 0.1 collective-permute-done.4
  511.3 4.1 collective-permute-done.5
  515.5 2.3 convolution_bitcast_fusion.2
  517.7 0.1 fusion.12
  517.8 4.0 collective-permute-start.6
  521.8 1.3 collective-permute-start.7
  523.1 0.3 collective-permute-done.6
  523.5 4.1 collective-permute-done.7
  527.7 2.3 convolution_bitcast_fusion.1
  530.0 0.0 copy-start.2
  530.0 13.3 %convolution_bitcast_fusion = f32[88,64,128]{2,1,0:T(8,128)} fusion(bf16[88,128,1024]{2,1,0:T(8,128)(2,1)} %bitcast.196, f32[64,1024]{1,0:T(8,128)S(1)} %fusion.10), kind=kOutput, calls=%fused_computation.4 | convolution fusion | flops 1476460544 | bytes 26214400 | tf_op jit(solution)/shard_map/dp,skp->sdk/dot_general | solution.py:63
  543.3 0.0 copy-done.2
  543.3 0.0 copy-start.3
  543.3 0.0 reduce-scatter.2.cloned.1.call-update
  543.4 0.6 copy-done.3
  544.0 0.1 dynamic_slice.3
  544.1 0.1 iota_compare_fusion.2
  544.1 45.3 %reduce-scatter.2.cloned.1.call-done = f32[11,64,128]{2,1,0:T(8,128)} async-done(((f32[88,64,128]{2,1,0:T(8,128)}), f32[11,64,128]{2,1,0:T(8,128)}) %reduce-scatter.2.cloned.1.call-update) | async-done | bytes 360464 | tf_op jit(solution)/shard_map/reduce_scatter | solution.py:62
  589.5 1.7 select_convert_fusion.1
  (43 shorter events, 0.5 us)
Async XLA Ops:
  7.2 335.4 %copy-start = (f32[1024,384]{1,0:T(8,128)S(1)}, f32[1024,384]{1,0:T(8,128)}, u32[]{:S(2)}) copy-start(f32[1024,384]{1,0:T(8,128)} %param.9) | copy-start | bytes 4718596
  7.2 316.3 %all-gather.2.cloned.1.call-start = ((), (), s32[]{:S(2)}) async-start(), calls=%async_computation.1 | async-start | bytes 8454144 | tf_op jit(solution)/shard_map/all_gather | solution.py:51
  7.9 473.3 %all-reduce.2.cloned.1.call-start = ((), (), s32[]{:S(2)}) async-start(), calls=%async_computation.2 | async-start | bytes 524288 | tf_op jit(solution)/shard_map/psum | solution.py:58
  342.5 247.0 %reduce-scatter.2.cloned.1.call-start = ((), (), s32[]{:S(2)}) async-start(), calls=%async_computation.3 | async-start | bytes 3244032 | tf_op jit(solution)/shard_map/reduce_scatter | solution.py:62
  482.2 5.0 collective-permute-start
  485.7 5.8 collective-permute-start.1
  487.3 6.4 %copy-start.1 = (f32[64,1024]{1,0:T(8,128)S(1)}, f32[64,1024]{1,0:T(8,128)}, u32[]{:S(2)}) copy-start(f32[64,1024]{1,0:T(8,128)} %all-reduce.2.cloned.1.call-done) | copy-start | bytes 786436
  493.8 5.1 collective-permute-start.2
  497.3 5.8 collective-permute-start.3
  505.5 5.7 collective-permute-start.4
  509.6 5.8 collective-permute-start.5
  517.8 5.6 collective-permute-start.6
  521.8 5.8 collective-permute-start.7
  530.0 13.3 %copy-start.2 = (f32[64,1024]{1,0:T(8,128)}, f32[64,1024]{1,0:T(8,128)S(1)}, u32[]{:S(2)}) copy-start(f32[64,1024]{1,0:T(8,128)S(1)} %fusion.10) | copy-start | bytes 786436
  543.3 0.7 copy-start.3
Sparse Core Ops, SparseCore 0:
  9.7 313.7 all-gather.1
  342.6 138.5 all-reduce.1
  543.5 45.9 reduce-scatter.1
where the time goes:
time: 598 us
  waiting for transfers between devices  508 us (85%)
  matrix products  41.3 us (7%)
  starting transfers between devices  20.5 us (3%)
  between operations  14.2 us (2%)
  local copies, waits for them, and re-layouts  9.59 us (2%)
    all_gather x1, waiting for transfers between devices, shards(): shard_piece = lax.all_gather(density, ('pair', 'aux'), axis=0, tiled=True)  315 us
    psum x1, waiting for transfers between devices, shards(): fit_total = lax.psum(partial_fit, 'pair')  130 us
    reduce_scatter x1, waiting for transfers between devices, shards(): lax.psum_scatter(jnp.einsum('dp,skp->sdk', coeff_b, tensor, preferred_ele...  45.3 us
    ppermute x4, waiting for transfers between devices, padded_2(): after = lax.ppermute(first, axis, down)  16.5 us
    ppermute x4, starting transfers between devices, padded_2(): before = lax.ppermute(last, axis, up)  15.1 us
    dot_general x1, matrix products, shards(): jnp.einsum('dp,skp->sdk', coeff_b, tensor, preferred_element_type=jnp.flo...  13.3 us
  transfers between devices with their start and end apart: 11, of which 11 were waited for; matrix products, arithmetic and copies ran while one was open for 2% of the time, Pallas kernels for 0%

commit v1 on v0

v1 whole, which is shorter than its diff:
```python
import jax
import jax.numpy as jnp
from jax import lax
from jax.experimental import pallas as pl
from jax.experimental.pallas import tpu as pltpu
from jax.sharding import PartitionSpec as P

F32 = jnp.float32
BF16 = jnp.bfloat16
BS = 128
HB = 128
ND = 64
SLOTS = 88
OWN = 11
AUX = 1024
HALF = 512
ROWS = SLOTS * BS
CHUNK = 1024
NCHUNK = ROWS // CHUNK

PARTS = (
    (0, 6, 0, (0, 1, 2)),
    (6, 5, 768, (1, 2, 0)),
    (11, 5, 1408, (2, 0, 1)),
)


def mod(value, size):
    return lax.rem(value + size, size)


def kernel(block_list, block_sizes, density, slab, metric, coulomb, coeffs, *scratch):
    (slab_v, held, picked, acc, sib_acc, fit_send, fit_recv, mw, wh, wl, u0, u, lh,
     own_u, halo, call, cb, opp_send, opp_recv, nb_send, nb_recv, x_send, x_recv, mine,
     index, slab_sem, local_sem, send_sem, recv_sem) = scratch

    pair = lax.axis_index("pair")
    aux = lax.axis_index("aux")
    core = lax.rem(pair, 2)
    chip = pair // 2
    x = (chip // 4) * 2 + aux // 4
    y = lax.rem(chip, 4)
    z = lax.rem(aux, 4)

    def device(coords, at_core):
        ax, ay, az = coords
        return (((ax // 2) * 4 + ay) * 2 + at_core, lax.rem(ax, 2) * 4 + az)

    def moved(dim, by):
        coords = [x, y, z]
        coords[dim] = mod(coords[dim] + by, 4)
        return device(coords, core)

    sibling = device([x, y, z], 1 - core)
    ext_aux = mod(aux + 2 * core - 1, 8)
    ext = (chip * 2 + (1 - core), ext_aux)
    chips = [(mod(chip + o, 8) * 2 + core, aux) for o in range(1, 8)]
    x_mate = (pair, mod(aux + 4, 8))

    slab_copies = []
    for n in range(NCHUNK):
        rows = pl.ds(n * CHUNK, CHUNK)
        slab_copies.append(pltpu.make_async_copy(slab.at[rows, :], slab_v.at[rows, :], slab_sem.at[n]))

    own_metric = pltpu.make_async_copy(
        metric.at[pl.ds(pl.multiple_of(core * 128, 128), 896), :],
        mw.at[pl.ds(pl.multiple_of(384 - core * 384, 128), 896), :],
        local_sem.at[0],
    )
    own_metric.start()

    def place(part, i3, i2, i1, at_core):
        _, tiles, base, _ = PARTS[part]
        return base + (((at_core * 4 + i3) * 4 + i2) * 4 + i1) * tiles

    def spot(part):
        order = PARTS[part][3]
        coords = (x, y, z)
        return coords[order[0]], coords[order[1]], coords[order[2]]

    own_tiles = []
    for part, (first, tiles, _, _) in enumerate(PARTS):
        i1, i2, i3 = spot(part)
        copy = pltpu.make_async_copy(
            density.at[pl.ds(first, tiles)],
            held.at[pl.ds(place(part, i3, i2, i1, core), tiles)],
            local_sem.at[1 + part],
        )
        copy.start()
        own_tiles.append(copy)
    for copy in slab_copies:
        copy.start()

    barrier = pltpu.get_barrier_semaphore()
    partners = [moved(d, s) for d in range(3) for s in (1, -1)] + [sibling, ext, x_mate] + chips
    for partner in partners:
        pl.semaphore_signal(barrier, inc=1, device_id=partner, device_id_type=pl.DeviceIdType.MESH)
    pl.semaphore_wait(barrier, len(partners))

    count = [0]
    sent = []

    def send(src, dst, to):
        n = count[0]
        count[0] += 1
        copy = pltpu.make_async_remote_copy(
            src_ref=src, dst_ref=dst, send_sem=send_sem.at[n], recv_sem=recv_sem.at[n],
            device_id=to, device_id_type=pl.DeviceIdType.MESH,
        )
        copy.start()
        sent.append(copy)
        return n

    def arrived(n, ref):
        pltpu.make_async_remote_copy(
            src_ref=ref, dst_ref=ref, send_sem=send_sem.at[n], recv_sem=recv_sem.at[n],
            device_id=sibling, device_id_type=pl.DeviceIdType.MESH,
        ).wait_recv()

    def window(start, size):
        return held.at[pl.ds(start, size)]

    sib_waits = []

    def to_sibling(part, start, size):
        _, tiles, _, _ = PARTS[part]
        ref = window(start, size)
        n = send(ref, ref, sibling)
        other = start + (1 - 2 * core) * 64 * tiles
        sib_waits.append((n, window(other, size)))

    class Ring:
        def __init__(self, part, level, start_of, size, cut):
            self.part, self.start_of, self.size, self.cut = part, start_of, size, cut
            self.dim = PARTS[part][3][level]
            self.at = (x, y, z)[self.dim]

        def piece(self, by):
            return self.start_of(mod(self.at + by, 4))

        def start(self, src=None):
            ref = window(self.piece(0), self.size)
            src = ref if src is None else src
            self.up = send(src, ref, moved(self.dim, 1))
            self.down = send(src, ref, moved(self.dim, -1))

        def middle(self):
            arrived(self.up, window(self.piece(-1), self.size))
            low = window(self.piece(-1), self.cut)
            self.up_far = send(low, low, moved(self.dim, 1))
            arrived(self.down, window(self.piece(1), self.size))
            high = window(self.piece(1) + self.cut, self.size - self.cut)
            self.down_far = send(high, high, moved(self.dim, -1))

        def end(self):
            arrived(self.up_far, window(self.piece(2), self.cut))
            arrived(self.down_far, window(self.piece(2) + self.cut, self.size - self.cut))

        def share(self, *bys):
            for by in bys:
                to_sibling(self.part, self.piece(by), self.size)

    first_rings, second_rings, third_rings = [], [], []
    for part in range(3):
        first, tiles, _, _ = PARTS[part]
        i1, i2, i3 = spot(part)
        first_rings.append(Ring(part, 0, lambda i, part=part, i2=i2, i3=i3: place(part, i3, i2, i, core),
                                tiles, tiles // 2))
        second_rings.append(Ring(part, 1, lambda i, part=part, i3=i3: place(part, i3, i, 0, core),
                                 4 * tiles, 2 * tiles))
        third_rings.append({
            by: Ring(part, 2, lambda i, part=part, i2=i2, by=by: place(part, i, mod(i2 + by, 4), 0, core),
                     4 * tiles, 2 * tiles)
            for by in (0, -1, 1, 2)
        })

    for part, ring in enumerate(first_rings):
        first, tiles, _, _ = PARTS[part]
        ring.start(density.at[pl.ds(first, tiles)])
    def find(s, _):
        b = block_list[s]
        j = b & 3
        bz = (b >> 2) & 3
        blo = (b >> 4) & 1
        bc = (b >> 5) & 1
        by = (b >> 6) & 3
        bx = ((b >> 8) & 1) * 2 + blo
        places = (
            (((bc * 4 + bz) * 4 + by) * 4 + bx) * 6,
            768 + (((bc * 4 + bx) * 4 + bz) * 4 + by) * 5 - 6,
            1408 + (((bc * 4 + by) * 4 + bx) * 4 + bz) * 5 - 11,
        )
        for r in range(4):
            t = j * 4 + r
            index[s * 4 + r] = t + jnp.where(t < 6, places[0], jnp.where(t < 11, places[1], places[2]))
        return 0

    for ring in first_rings:
        ring.middle()
    for ring in first_rings:
        ring.end()
    for copy in own_tiles:
        copy.wait()
    for part in range(3):
        second_rings[part].start()
        third_rings[part][0].start()
        second_rings[part].share(0)
    for part in range(3):
        second_rings[part].middle()
        third_rings[part][-1].start()
        third_rings[part][1].start()
        second_rings[part].share(-1, 1)
    for part in range(3):
        second_rings[part].end()
        third_rings[part][2].start()
        second_rings[part].share(2)
    metric_n = send(
        metric.at[pl.ds(pl.multiple_of(core * 640, 128), 384), :],
        mw.at[pl.ds(pl.multiple_of(896 - core * 896, 128), 384), :],
        ext,
    )
    lax.fori_loop(0, SLOTS, find, 0)
    for part in range(3):
        third_rings[part][0].middle()
        third_rings[part][0].share(-1, 1)
    for by in (-1, 1):
        for part in range(3):
            third_rings[part][by].middle()
            third_rings[part][by].share(-1, 1)
    for part in range(3):
        third_rings[part][0].end()
        third_rings[part][0].share(2)
    for part in range(3):
        third_rings[part][2].middle()
        third_rings[part][2].share(-1, 1)
    for by in (-1, 1):
        for part in range(3):
            third_rings[part][by].end()
            third_rings[part][by].share(2)
    for part in range(3):
        third_rings[part][2].end()
        third_rings[part][2].share(2)

    own_metric.wait()
    arrived(metric_n, mw.at[pl.ds(pl.multiple_of(core * 896, 128), 384), :])
    eye = (lax.broadcasted_iota(jnp.int32, (HB, HB), 0) == lax.broadcasted_iota(jnp.int32, (HB, HB), 1))
    low_ok = jnp.logical_or(aux > 0, core == 1)
    high_ok = jnp.logical_or(aux < 7, core == 0)
    zero_block = jnp.zeros((HB, HB), BF16)

    def build(i, _):
        for half in range(2):
            n = 2 * i + half
            rows = pl.ds(pl.multiple_of(n * HB, HB), HB)
            middle = mw[rows, HB:2 * HB]
            diag = jnp.sum(jnp.where(eye, middle, 0.0), axis=1, keepdims=True)
            keep = jnp.logical_and(jnp.logical_or(n > 2, low_ok), jnp.logical_or(n < 7, high_ok))
            scale = jnp.where(keep, -1.0 / diag, 0.0)
            for k in range(3):
                block = mw[rows, k * HB:(k + 1) * HB]
                if k == 1:
                    block = jnp.where(eye, 0.0, block)
                block = (block * scale).T
                high = block.astype(BF16)
                low = (block - high.astype(F32)).astype(BF16)
                at = (k + half) * HB
                wh[i, at:at + HB, half * HB:(half + 1) * HB] = high
                wl[i, at:at + HB, half * HB:(half + 1) * HB] = low
            at = (3 - 3 * half) * HB
            wh[i, at:at + HB, half * HB:(half + 1) * HB] = zero_block
            wl[i, at:at + HB, half * HB:(half + 1) * HB] = zero_block
        return 0

    lax.fori_loop(0, 5, build, 0)
    diag_rows = []
    for n in range(3, 7):
        middle = mw[n * HB:(n + 1) * HB, HB:2 * HB]
        diag_rows.append(jnp.sum(jnp.where(eye, middle, 0.0), axis=0, keepdims=True))
    diag_row = jnp.concatenate(diag_rows, axis=1)

    for n, ref in sib_waits:
        arrived(n, ref)

    lane = lax.broadcasted_iota(jnp.int32, (16, BS), 1)

    def pick(s, _):
        live = jnp.where(lane < block_sizes[s], 1.0, 0.0).astype(BF16)
        column = pl.ds(pl.multiple_of(s * BS, BS), BS)
        for r in range(4):
            picked[r * 16:(r + 1) * 16, column] = held[index[s * 4 + r]] * live
        return 0

    lax.fori_loop(0, SLOTS, pick, 0)

    for copy in slab_copies:
        copy.wait()

    def fit(out, half):
        columns = pl.ds(pl.multiple_of(half * HALF, HALF), HALF)

        def step(n, _):
            rows = pl.ds(pl.multiple_of(n * CHUNK, CHUNK), CHUNK)
            term = jnp.dot(picked[:, rows], slab_v[rows, columns], preferred_element_type=F32)

            @pl.when(n == 0)
            def _():
                out[...] = term

            @pl.when(n > 0)
            def _():
                out[...] += term

            return 0

        lax.fori_loop(0, NCHUNK, step, 0)

    fit(sib_acc.at[0], 1 - core)
    n = send(sib_acc.at[0], sib_acc.at[1], sibling)
    fit(acc, core)
    arrived(n, sib_acc.at[1])
    for q in range(8):
        fit_send[q] = acc[q * 8:(q + 1) * 8, :] + sib_acc[1, q * 8:(q + 1) * 8, :]
    waits = []
    for o in range(1, 8):
        to = mod(chip + o, 8)
        n = send(fit_send.at[to], fit_recv.at[o], chips[o - 1])
        waits.append((n, fit_recv.at[o]))
    total = fit_send[chip]
    for o, (n, ref) in enumerate(waits):
        arrived(n, ref)
        total = total + fit_recv[o + 1]

    own_u[...] = total / diag_row
    n_sib = send(own_u, halo.at[core], sibling)
    n_ext = send(own_u, halo.at[1 - core], ext)
    u0[:, HALF:2 * HALF] = own_u[...]
    arrived(n_sib, halo.at[1 - core])
    arrived(n_ext, halo.at[core])
    u0[:, :HALF] = jnp.where(low_ok, halo[0], 0.0)
    u0[:, 2 * HALF:] = jnp.where(high_ok, halo[1], 0.0)
    u[...] = u0[...]
    for pairs in ((0, 1, 2, 3, 4), (0, 1, 2, 3, 4), (1, 2, 3), (1, 2, 3)):
        values = u[...]
        high = values.astype(BF16)
        lh[0:8, :] = values
        lh[8:16, :] = values - high.astype(F32)
        for i in pairs:
            left = lh[:, i * 256:i * 256 + 512].astype(BF16)
            one = jnp.dot(left, wh[i], preferred_element_type=F32)
            two = jnp.dot(left, wl[i], preferred_element_type=F32)
            cols = slice((2 * i + 1) * HB, (2 * i + 3) * HB)
            u[:, cols] = u0[:, cols] + (one[0:8] + (one[8:16] + two[0:8]))

    call[core, chip] = u[:, HALF:2 * HALF]
    own_ref = call.at[core, chip]
    waits = []
    n_own = send(own_ref, own_ref, sibling)
    for o in range(1, 8):
        waits.append((send(own_ref, own_ref, chips[o - 1]), call.at[core, mod(chip - o, 8)]))
    shared = [(n_own, call.at[1 - core, chip])]
    for o, (n, ref) in enumerate(waits):
        arrived(n, ref)
        shared.append((send(ref, ref, sibling), call.at[1 - core, mod(chip - o - 1, 8)]))
    for n, ref in shared:
        arrived(n, ref)
    for half in range(2):
        for q in range(4):
            value = jnp.concatenate([call[half, 2 * q], call[half, 2 * q + 1]], axis=0)
            coeffs[q * 16:(q + 1) * 16, half * HALF:(half + 1) * HALF] = value
            cb[q * 16:(q + 1) * 16, half * HALF:(half + 1) * HALF] = value.astype(BF16)

    def coulomb_part(to, store):
        def dots(start, slots):
            rows = pl.ds(pl.multiple_of((to * OWN + start) * BS, BS), slots * BS)
            out = lax.dot_general(cb[...], slab_v[rows, :], (((1,), (1,)), ((), ())),
                                  preferred_element_type=F32)
            for k in range(slots):
                store(start + k, out[:, k * BS:(k + 1) * BS])

        def two(i, _):
            dots(2 * i, 2)
            return 0

        lax.fori_loop(0, OWN // 2, two, 0)
        dots(OWN - 1, 1)

    def into(ref, *terms):
        def store(i, value):
            for term in terms:
                value = value + term[i].astype(F32)
            ref[i] = value.astype(ref.dtype)
        return store

    up, down = moved(2, 1), moved(2, -1)
    z_up, z_down, z_far = mod(z + 1, 4), mod(z - 1, 4), mod(z + 2, 4)
    coulomb_part(z_far, into(opp_send.at[0]))
    n_a = send(opp_send.at[0], opp_recv.at[0], up)
    coulomb_part(4 + z_far, into(opp_send.at[1]))
    n_b = send(opp_send.at[1], opp_recv.at[1], down)
    waits = []

    def neighbour(to, k, into_store, target):
        coulomb_part(to, into_store)
        waits.append((send(nb_send.at[k], nb_recv.at[k], target), nb_recv.at[k]))

    neighbour(4 + z_up, 0, into(nb_send.at[0]), up)
    neighbour(z_down, 1, into(nb_send.at[1]), down)
    arrived(n_a, opp_recv.at[0])
    neighbour(z_up, 2, into(nb_send.at[2], opp_recv.at[0]), up)
    arrived(n_b, opp_recv.at[1])
    neighbour(4 + z_down, 3, into(nb_send.at[3], opp_recv.at[1]), down)
    lo = aux // 4
    other = 1 - lo
    coulomb_part(other * 4 + z, into(mine.at[1]))
    coulomb_part(lo * 4 + z, into(mine.at[0]))
    for n, ref in waits:
        arrived(n, ref)
    for i in range(OWN):
        value = mine[1, i] + nb_recv[2 - 2 * other, i].astype(F32) + nb_recv[1 + 2 * other, i].astype(F32)
        x_send[i] = value.astype(BF16)
    n_x = send(x_send, x_recv, x_mate)
    for i in range(OWN):
        mine[0, i] = mine[0, i] + nb_recv[2 - 2 * lo, i].astype(F32) + nb_recv[1 + 2 * lo, i].astype(F32)
    arrived(n_x, x_recv)
    row_lane = lax.broadcasted_iota(jnp.int32, (ND, BS), 1)
    for i in range(OWN):
        value = mine[0, i] + x_recv[i].astype(F32)
        live = row_lane < block_sizes[aux * OWN + i]
        coulomb[i] = jnp.where(live, value, 0.0).astype(BF16)

    for copy in sent:
        copy.wait_send()


NSEMS = 180


def shards(slab, density, block_list, block_sizes, metric):
    vmem = pl.BlockSpec(memory_space=pltpu.VMEM)
    smem = pl.BlockSpec(memory_space=pltpu.SMEM)
    hbm = pl.BlockSpec(memory_space=pl.ANY)
    coulomb, coeffs = pl.pallas_call(
        kernel,
        out_shape=(
            jax.ShapeDtypeStruct((OWN, ND, BS), BF16),
            jax.ShapeDtypeStruct((ND, AUX), F32),
        ),
        in_specs=[smem, smem, hbm, hbm, hbm],
        out_specs=(vmem, vmem),
        scratch_shapes=[
            pltpu.VMEM((ROWS, AUX), BF16),
            pltpu.VMEM((2048, 16, BS), BF16),
            pltpu.VMEM((ND, ROWS), BF16),
            pltpu.VMEM((ND, HALF), F32),
            pltpu.VMEM((2, ND, HALF), F32),
            pltpu.VMEM((8, 8, HALF), F32),
            pltpu.VMEM((8, 8, HALF), F32),
            pltpu.VMEM((1280, 3 * HB), F32),
            pltpu.VMEM((5, 512, 256), BF16),
            pltpu.VMEM((5, 512, 256), BF16),
            pltpu.VMEM((8, 3 * HALF), F32),
            pltpu.VMEM((8, 3 * HALF), F32),
            pltpu.VMEM((16, 3 * HALF), F32),
            pltpu.VMEM((8, HALF), F32),
            pltpu.VMEM((2, 8, HALF), F32),
            pltpu.VMEM((2, 8, 8, HALF), F32),
            pltpu.VMEM((ND, AUX), BF16),
            pltpu.VMEM((2, OWN, ND, BS), BF16),
            pltpu.VMEM((2, OWN, ND, BS), BF16),
            pltpu.VMEM((4, OWN, ND, BS), BF16),
            pltpu.VMEM((4, OWN, ND, BS), BF16),
            pltpu.VMEM((OWN, ND, BS), BF16),
            pltpu.VMEM((OWN, ND, BS), BF16),
            pltpu.VMEM((2, OWN, ND, BS), F32),
            pltpu.SMEM((4 * SLOTS,), jnp.int32),
            pltpu.SemaphoreType.DMA((NCHUNK,)),
            pltpu.SemaphoreType.DMA((4,)),
            pltpu.SemaphoreType.DMA((NSEMS,)),
            pltpu.SemaphoreType.DMA((NSEMS,)),
        ],
        compiler_params=pltpu.CompilerParams(
            collective_id=0, has_side_effects=True, vmem_limit_bytes=56 * 1024 * 1024
        ),
        cost_estimate=pl.CostEstimate(flops=4 * ND * ROWS * AUX, bytes_accessed=2 * ROWS * AUX, transcendentals=0),
    )(block_list, block_sizes, density.reshape(16, 16, BS), slab, metric)
    return coulomb, coeffs


def solution(mesh):
    return jax.shard_map(
        shards,
        mesh=mesh,
        in_specs=(
            P("pair", "aux"),
            P(("pair", "aux"), None, None),
            P("pair"),
            P("pair"),
            P("aux", None),
        ),
        out_specs=(P(("pair", "aux"), None, None), P(None, "aux")),
        check_vma=False,
    )
```

time: 598 us -> 100 us (0.17)
  waiting for transfers between devices: 508 us -> 0 us
  Pallas kernels: 0 us -> 95.4 us
  matrix products: 41.3 us -> 0 us
  starting transfers between devices: 20.5 us -> 0 us
  between operations: 14.2 us -> 0.64 us
  local copies, waits for them, and re-layouts: 9.59 us -> 3.28 us
    all_gather x1 -> x0, waiting for transfers between devices: 315 us -> none  [shards(): shard_piece = lax.all_gather(density, ('pair', 'aux'), axis=0, tiled=True)]
    psum x1 -> x0, waiting for transfers between devices: 130 us -> none  [shards(): fit_total = lax.psum(partial_fit, 'pair')]
    pallas_call x0 -> x1, Pallas kernels: none -> 95.4 us  [shards(): pl.pallas_call(kernel, out_shape=(jax.ShapeDtypeStruct((OWN, ND, BS), BF1...]
    reduce_scatter x1 -> x0, waiting for transfers between devices: 45.3 us -> none  [shards(): lax.psum_scatter(jnp.einsum('dp,skp->sdk', coeff_b, tensor, preferred_ele...]
    dot_general x7 -> x0, matrix products: 41.3 us -> none  [the longest x1 13.3 us: shards(): jnp.einsum('dp,skp->sdk', coeff_b, tensor, preferred_element_type=jnp.flo...]
    ppermute x8 -> x0, starting transfers between devices: 20.4 us -> none  [the longest x4 15.1 us: padded_2(): before = lax.ppermute(last, axis, up)]
    ppermute x8 -> x0, waiting for transfers between devices: 17.4 us -> none  [the longest x4 16.5 us: padded_2(): after = lax.ppermute(first, axis, down)]
    gather x1 -> x0, local copies, waits for them, and re-layouts: 8.6 us -> none  [jacobi_solve(): jnp.take_along_axis(metric, (HB + row_index % HB)[:, None], axis=1)[:, 0]]
  transfers between devices with their start and end apart: 11 -> 0, of which waited for: 11 -> 0; matrix products, arithmetic and copies ran while one was open for 2% -> 0% of each run, Pallas kernels for 0% -> 0%
where the time goes in v1:
time: 100 us; the launch traced here: 99.3 us
  Pallas kernels  95.4 us (95%)
  local copies, waits for them, and re-layouts  3.28 us (3%)
    pallas_call x1, Pallas kernels, shards(): pl.pallas_call(kernel, out_shape=(jax.ShapeDtypeStruct((OWN, ND, BS), BF1...  95.4 us
    unnamed x2, local copies, waits for them, and re-layouts  3.28 us

profile of v1, /device:TPU:0, one launch (start us, length us, event | category | flops | bytes accessed | tf_op | source)
XLA Modules:
  0.0 99.3 jit_solution(11159654063286404200)
XLA Ops:
  0.6 95.4 %shard_map.68 = (bf16[11,64,128]{2,1,0:T(8,128)(2,1)}, f32[64,1024]{1,0:T(8,128)}) custom-call(s32[88]{0:T(128)} %block_list.1, s32[88]{0:T(128)} %block_sizes.1, bf16[16,16,128]{2,1,0:T(8,128)(2,1)} %bitcast.1, bf16[11264,1024]{1,0:T(8,128)(2,1)} %slab.1, f32[1024,384]{1,0:T(8,128)} %metric.1), custom_call_target="tpu_custom_call" | custom-call | flops 2952790016 | bytes 23068672 | tf_op jit(solution)/shard_map/pallas_call | solution.py:442
  96.0 1.6 %copy.9 = bf16[11,64,128]{2,1,0:T(8,128)(2,1)} copy(bf16[11,64,128]{2,1,0:T(8,128)(2,1)} %get-tuple-element.4) | data formatting | bytes 360448
  97.6 1.7 %copy.10 = f32[64,1024]{1,0:T(8,128)} copy(f32[64,1024]{1,0:T(8,128)} %get-tuple-element.5) | data formatting | bytes 524288

commit v2 on v1

--- a/solution.py
+++ b/solution.py
@@ -15,6 +15,8 @@
 AUX = 1024
 HALF = 512
 ROWS = SLOTS * BS
+XS = 5
+ZS = OWN - XS
 CHUNK = 1024
 NCHUNK = ROWS // CHUNK
 
@@ -31,8 +33,8 @@
 
 def kernel(block_list, block_sizes, density, slab, metric, coulomb, coeffs, *scratch):
     (slab_v, held, picked, acc, sib_acc, fit_send, fit_recv, mw, wh, wl, u0, u, lh,
-     own_u, halo, call, cb, opp_send, opp_recv, nb_send, nb_recv, x_send, x_recv, mine,
-     index, slab_sem, local_sem, send_sem, recv_sem) = scratch
+     own_u, halo, call, cb, zfar_send, zfar_recv, znb_send, znb_recv, zx_send, zx_recv, z_mine,
+     xs_send, xs_recv, xfar_send, xfar_recv, xnb_send, xnb_recv, x_mine, index, slab_sem, local_sem, send_sem, recv_sem) = scratch
 
     pair = lax.axis_index("pair")
     aux = lax.axis_index("aux")
@@ -46,16 +48,27 @@
         ax, ay, az = coords
         return (((ax // 2) * 4 + ay) * 2 + at_core, lax.rem(ax, 2) * 4 + az)
 
+    moves = {}
+    for dim in range(3):
+        for by in (1, -1, 2):
+            coords = [x, y, z]
+            coords[dim] = mod(coords[dim] + by, 4)
+            moves[dim, by] = device(coords, core)
+
     def moved(dim, by):
-        coords = [x, y, z]
-        coords[dim] = mod(coords[dim] + by, 4)
-        return device(coords, core)
+        return moves[dim, by]
 
     sibling = device([x, y, z], 1 - core)
     ext_aux = mod(aux + 2 * core - 1, 8)
     ext = (chip * 2 + (1 - core), ext_aux)
     chips = [(mod(chip + o, 8) * 2 + core, aux) for o in range(1, 8)]
     x_mate = (pair, mod(aux + 4, 8))
+
+    barrier = pltpu.get_barrier_semaphore()
+    partners = [moves[0, 1], moves[0, -1], moves[2, 1], moves[2, -1], moves[2, 2], sibling, ext]
+    partners += chips + [(mod(chip + o, 8) * 2 + 1 - core, aux) for o in range(1, 8)]
+    for partner in partners:
+        pl.semaphore_signal(barrier, inc=1, device_id=partner, device_id_type=pl.DeviceIdType.MESH)
 
     slab_copies = []
     for n in range(NCHUNK):
@@ -88,14 +101,10 @@
         )
         copy.start()
         own_tiles.append(copy)
-    for copy in slab_copies:
-        copy.start()
-
-    barrier = pltpu.get_barrier_semaphore()
-    partners = [moved(d, s) for d in range(3) for s in (1, -1)] + [sibling, ext, x_mate] + chips
-    for partner in partners:
-        pl.semaphore_signal(barrier, inc=1, device_id=partner, device_id_type=pl.DeviceIdType.MESH)
+
     pl.semaphore_wait(barrier, len(partners))
+    for copy in own_tiles:
+        copy.wait()
 
     count = [0]
     sent = []
@@ -130,7 +139,7 @@
         sib_waits.append((n, window(other, size)))
 
     class Ring:
-        def __init__(self, part, level, start_of, size, cut):
+        def __init__(self, part, level, start_of, size, cut=0):
             self.part, self.start_of, self.size, self.cut = part, start_of, size, cut
             self.dim = PARTS[part][3][level]
             self.at = (x, y, z)[self.dim]
@@ -143,9 +152,14 @@
             src = ref if src is None else src
             self.up = send(src, ref, moved(self.dim, 1))
             self.down = send(src, ref, moved(self.dim, -1))
+            if self.cut == 0:
+                self.far = send(src, ref, moved(self.dim, 2))
 
         def middle(self):
             arrived(self.up, window(self.piece(-1), self.size))
+            if self.cut == 0:
+                arrived(self.down, window(self.piece(1), self.size))
+                return
             low = window(self.piece(-1), self.cut)
             self.up_far = send(low, low, moved(self.dim, 1))
             arrived(self.down, window(self.piece(1), self.size))
@@ -153,6 +167,9 @@
             self.down_far = send(high, high, moved(self.dim, -1))
 
         def end(self):
+            if self.cut == 0:
+                arrived(self.far, window(self.piece(2), self.size))
+                return
             arrived(self.up_far, window(self.piece(2), self.cut))
             arrived(self.down_far, window(self.piece(2) + self.cut, self.size - self.cut))
 
@@ -165,9 +182,9 @@
         first, tiles, _, _ = PARTS[part]
         i1, i2, i3 = spot(part)
         first_rings.append(Ring(part, 0, lambda i, part=part, i2=i2, i3=i3: place(part, i3, i2, i, core),
-                                tiles, tiles // 2))
+                                tiles))
         second_rings.append(Ring(part, 1, lambda i, part=part, i3=i3: place(part, i3, i, 0, core),
-                                 4 * tiles, 2 * tiles))
+                                 4 * tiles))
         third_rings.append({
             by: Ring(part, 2, lambda i, part=part, i2=i2, by=by: place(part, i, mod(i2 + by, 4), 0, core),
                      4 * tiles, 2 * tiles)
@@ -176,7 +193,10 @@
 
     for part, ring in enumerate(first_rings):
         first, tiles, _, _ = PARTS[part]
-        ring.start(density.at[pl.ds(first, tiles)])
+        ring.start()
+    for copy in slab_copies:
+        copy.start()
+
     def find(s, _):
         b = block_list[s]
         j = b & 3
@@ -199,56 +219,32 @@
         ring.middle()
     for ring in first_rings:
         ring.end()
-    for copy in own_tiles:
-        copy.wait()
     for part in range(3):
         second_rings[part].start()
+    for part in range(3):
         third_rings[part][0].start()
+    for part in range(3):
         second_rings[part].share(0)
     for part in range(3):
         second_rings[part].middle()
+    for part in range(3):
         third_rings[part][-1].start()
         third_rings[part][1].start()
+    for part in range(3):
         second_rings[part].share(-1, 1)
     for part in range(3):
         second_rings[part].end()
+    for part in range(3):
         third_rings[part][2].start()
+    for part in range(3):
         second_rings[part].share(2)
-    metric_n = send(
-        metric.at[pl.ds(pl.multiple_of(core * 640, 128), 384), :],
-        mw.at[pl.ds(pl.multiple_of(896 - core * 896, 128), 384), :],
-        ext,
-    )
     lax.fori_loop(0, SLOTS, find, 0)
-    for part in range(3):
-        third_rings[part][0].middle()
-        third_rings[part][0].share(-1, 1)
-    for by in (-1, 1):
-        for part in range(3):
-            third_rings[part][by].middle()
-            third_rings[part][by].share(-1, 1)
-    for part in range(3):
-        third_rings[part][0].end()
-        third_rings[part][0].share(2)
-    for part in range(3):
-        third_rings[part][2].middle()
-        third_rings[part][2].share(-1, 1)
-    for by in (-1, 1):
-        for part in range(3):
-            third_rings[part][by].end()
-            third_rings[part][by].share(2)
-    for part in range(3):
-        third_rings[part][2].end()
-        third_rings[part][2].share(2)
-
-    own_metric.wait()
-    arrived(metric_n, mw.at[pl.ds(pl.multiple_of(core * 896, 128), 384), :])
     eye = (lax.broadcasted_iota(jnp.int32, (HB, HB), 0) == lax.broadcasted_iota(jnp.int32, (HB, HB), 1))
     low_ok = jnp.logical_or(aux > 0, core == 1)
     high_ok = jnp.logical_or(aux < 7, core == 0)
     zero_block = jnp.zeros((HB, HB), BF16)
 
-    def build(i, _):
+    def build(i):
         for half in range(2):
             n = 2 * i + half
             rows = pl.ds(pl.multiple_of(n * HB, HB), HB)
@@ -271,12 +267,29 @@
             wl[i, at:at + HB, half * HB:(half + 1) * HB] = zero_block
         return 0
 
-    lax.fori_loop(0, 5, build, 0)
+
+    for by in (0, -1, 1, 2):
+        for part in range(3):
+            third_rings[part][by].middle()
+        for part in range(3):
+            third_rings[part][by].share(-1, 1)
+    own_metric.wait()
+    lax.fori_loop(0, 3, lambda i, _: build(2 - 2 * core + i), 0)
     diag_rows = []
     for n in range(3, 7):
         middle = mw[n * HB:(n + 1) * HB, HB:2 * HB]
         diag_rows.append(jnp.sum(jnp.where(eye, middle, 0.0), axis=0, keepdims=True))
     diag_row = jnp.concatenate(diag_rows, axis=1)
+    for by in (0, -1, 1, 2):
+        for part in range(3):
+            third_rings[part][by].end()
+        for part in range(3):
+            third_rings[part][by].share(2)
+    metric_n = send(
+        metric.at[pl.ds(pl.multiple_of(core * 640, 128), 384), :],
+        mw.at[pl.ds(pl.multiple_of(896 - core * 896, 128), 384), :],
+        ext,
+    )
 
     for n, ref in sib_waits:
         arrived(n, ref)
@@ -296,35 +309,28 @@
         copy.wait()
 
     def fit(out, half):
-        columns = pl.ds(pl.multiple_of(half * HALF, HALF), HALF)
-
         def step(n, _):
-            rows = pl.ds(pl.multiple_of(n * CHUNK, CHUNK), CHUNK)
-            term = jnp.dot(picked[:, rows], slab_v[rows, columns], preferred_element_type=F32)
-
-            @pl.when(n == 0)
-            def _():
-                out[...] = term
-
-            @pl.when(n > 0)
-            def _():
-                out[...] += term
-
+            columns = pl.ds(pl.multiple_of(half * HALF + n * 256, 256), 256)
+            out[n] = jnp.dot(picked[...], slab_v[:, columns], preferred_element_type=F32)
             return 0
 
-        lax.fori_loop(0, NCHUNK, step, 0)
+        lax.fori_loop(0, 2, step, 0)
 
     fit(sib_acc.at[0], 1 - core)
     n = send(sib_acc.at[0], sib_acc.at[1], sibling)
     fit(acc, core)
     arrived(n, sib_acc.at[1])
     for q in range(8):
-        fit_send[q] = acc[q * 8:(q + 1) * 8, :] + sib_acc[1, q * 8:(q + 1) * 8, :]
+        for n in range(2):
+            rows = slice(q * 8, (q + 1) * 8)
+            fit_send[q, :, n * 256:(n + 1) * 256] = acc[n, rows, :] + sib_acc[1, n, rows, :]
     waits = []
     for o in range(1, 8):
         to = mod(chip + o, 8)
         n = send(fit_send.at[to], fit_recv.at[o], chips[o - 1])
         waits.append((n, fit_recv.at[o]))
+    arrived(metric_n, mw.at[pl.ds(pl.multiple_of(core * 896, 128), 384), :])
+    lax.fori_loop(0, 2, lambda i, _: build(3 * core + i), 0)
     total = fit_send[chip]
     for o, (n, ref) in enumerate(waits):
         arrived(n, ref)
@@ -354,14 +360,12 @@
     call[core, chip] = u[:, HALF:2 * HALF]
     own_ref = call.at[core, chip]
     waits = []
-    n_own = send(own_ref, own_ref, sibling)
     for o in range(1, 8):
+        other = (mod(chip + o, 8) * 2 + 1 - core, aux)
         waits.append((send(own_ref, own_ref, chips[o - 1]), call.at[core, mod(chip - o, 8)]))
-    shared = [(n_own, call.at[1 - core, chip])]
-    for o, (n, ref) in enumerate(waits):
-        arrived(n, ref)
-        shared.append((send(ref, ref, sibling), call.at[1 - core, mod(chip - o - 1, 8)]))
-    for n, ref in shared:
+        waits.append((send(own_ref, own_ref, other), call.at[1 - core, mod(chip - o, 8)]))
+    waits.append((send(own_ref, own_ref, sibling), call.at[1 - core, chip]))
+    for n, ref in waits:
         arrived(n, ref)
     for half in range(2):
         for q in range(4):
@@ -369,64 +373,99 @@
             coeffs[q * 16:(q + 1) * 16, half * HALF:(half + 1) * HALF] = value
             cb[q * 16:(q + 1) * 16, half * HALF:(half + 1) * HALF] = value.astype(BF16)
 
-    def coulomb_part(to, store):
-        def dots(start, slots):
-            rows = pl.ds(pl.multiple_of((to * OWN + start) * BS, BS), slots * BS)
-            out = lax.dot_general(cb[...], slab_v[rows, :], (((1,), (1,)), ((), ())),
-                                  preferred_element_type=F32)
-            for k in range(slots):
-                store(start + k, out[:, k * BS:(k + 1) * BS])
-
-        def two(i, _):
-            dots(2 * i, 2)
-            return 0
-
-        lax.fori_loop(0, OWN // 2, two, 0)
-        dots(OWN - 1, 1)
-
-    def into(ref, *terms):
-        def store(i, value):
-            for term in terms:
-                value = value + term[i].astype(F32)
-            ref[i] = value.astype(ref.dtype)
-        return store
+    def dots(to, start, slots):
+        rows = pl.ds(pl.multiple_of(to * (OWN * BS) + start * BS, BS), slots * BS)
+        return lax.dot_general(cb[...], slab_v[rows, :], (((1,), (1,)), ((), ())),
+                               preferred_element_type=F32)
+
+    def put(ref, value, *terms):
+        slots = value.shape[1] // BS
+        for k in range(slots):
+            part = value[:, k * BS:(k + 1) * BS]
+            for term, first in terms:
+                if first <= k < first + term.shape[0]:
+                    part = part + term[k - first].astype(F32)
+            ref[k] = part.astype(ref.dtype)
+
+    def z_part(to):
+        return dots(to, XS, ZS)
+
+    def x_part(to):
+        return dots(to, 0, XS)
 
     up, down = moved(2, 1), moved(2, -1)
     z_up, z_down, z_far = mod(z + 1, 4), mod(z - 1, 4), mod(z + 2, 4)
-    coulomb_part(z_far, into(opp_send.at[0]))
-    n_a = send(opp_send.at[0], opp_recv.at[0], up)
-    coulomb_part(4 + z_far, into(opp_send.at[1]))
-    n_b = send(opp_send.at[1], opp_recv.at[1], down)
-    waits = []
-
-    def neighbour(to, k, into_store, target):
-        coulomb_part(to, into_store)
-        waits.append((send(nb_send.at[k], nb_recv.at[k], target), nb_recv.at[k]))
-
-    neighbour(4 + z_up, 0, into(nb_send.at[0]), up)
-    neighbour(z_down, 1, into(nb_send.at[1]), down)
-    arrived(n_a, opp_recv.at[0])
-    neighbour(z_up, 2, into(nb_send.at[2], opp_recv.at[0]), up)
-    arrived(n_b, opp_recv.at[1])
-    neighbour(4 + z_down, 3, into(nb_send.at[3], opp_recv.at[1]), down)
     lo = aux // 4
     other = 1 - lo
-    coulomb_part(other * 4 + z, into(mine.at[1]))
-    coulomb_part(lo * 4 + z, into(mine.at[0]))
-    for n, ref in waits:
-        arrived(n, ref)
-    for i in range(OWN):
-        value = mine[1, i] + nb_recv[2 - 2 * other, i].astype(F32) + nb_recv[1 + 2 * other, i].astype(F32)
-        x_send[i] = value.astype(BF16)
-    n_x = send(x_send, x_recv, x_mate)
-    for i in range(OWN):
-        mine[0, i] = mine[0, i] + nb_recv[2 - 2 * lo, i].astype(F32) + nb_recv[1 + 2 * lo, i].astype(F32)
-    arrived(n_x, x_recv)
+
+    put(zfar_send.at[0], z_part(z_far))
+    n_zfar0 = send(zfar_send.at[0], zfar_recv.at[0], up)
+    put(zfar_send.at[1], z_part(4 + z_far))
+    n_zfar1 = send(zfar_send.at[1], zfar_recv.at[1], down)
+    put(xs_send.at[0], x_part(other * 4 + z_far))
+    n_xs0 = send(xs_send.at[0], xs_recv.at[0], x_mate)
+    put(znb_send.at[0], z_part(4 + z_up))
+    n_znb0 = send(znb_send.at[0], znb_recv.at[0], up)
+    put(znb_send.at[1], z_part(z_down))
+    n_znb1 = send(znb_send.at[1], znb_recv.at[1], down)
+    put(xs_send.at[1], x_part(other * 4 + z_up))
+    n_xs1 = send(xs_send.at[1], xs_recv.at[1], x_mate)
+    put(xs_send.at[2], x_part(other * 4 + z_down))
+    n_xs2 = send(xs_send.at[2], xs_recv.at[2], x_mate)
+
+    arrived(n_xs0, xs_recv.at[0])
+    put(xfar_send, x_part(lo * 4 + z_far), (xs_recv.at[0], 0))
+    first, second = pl.ds(0, 2), pl.ds(2, XS - 2)
+    n_xfar0 = send(xfar_send.at[first], xfar_recv.at[first], up)
+    n_xfar1 = send(xfar_send.at[second], xfar_recv.at[second], down)
+    arrived(n_zfar0, zfar_recv.at[0])
+    put(znb_send.at[2], z_part(z_up), (zfar_recv.at[0], 0))
+    n_znb2 = send(znb_send.at[2], znb_recv.at[2], up)
+    arrived(n_zfar1, zfar_recv.at[1])
+    put(znb_send.at[3], z_part(4 + z_down), (zfar_recv.at[1], 0))
+    n_znb3 = send(znb_send.at[3], znb_recv.at[3], down)
+    put(xs_send.at[3], x_part(other * 4 + z))
+    n_xs3 = send(xs_send.at[3], xs_recv.at[3], x_mate)
+    put(z_mine.at[1], z_part(other * 4 + z))
+    arrived(n_xs1, xs_recv.at[1])
+    arrived(n_xfar0, xfar_recv.at[first])
+    put(xnb_send.at[0], x_part(lo * 4 + z_up), (xs_recv.at[1], 0), (xfar_recv.at[first], 0))
+    n_xnb0 = send(xnb_send.at[0], xnb_recv.at[0], up)
+    arrived(n_xs2, xs_recv.at[2])
+    arrived(n_xfar1, xfar_recv.at[second])
+    put(xnb_send.at[1], x_part(lo * 4 + z_down), (xs_recv.at[2], 0), (xfar_recv.at[second], 2))
+    n_xnb1 = send(xnb_send.at[1], xnb_recv.at[1], down)
+    put(z_mine.at[0], z_part(lo * 4 + z))
+    put(x_mine, x_part(lo * 4 + z))
+
+    for k, n in enumerate((n_znb0, n_znb1, n_znb2, n_znb3)):
+        arrived(n, znb_recv.at[k])
+
+    def z_sum(k, which, i):
+        return (z_mine[k, i] + znb_recv[2 - 2 * which, i].astype(F32)
+                + znb_recv[1 + 2 * which, i].astype(F32))
+
+    for i in range(ZS):
+        zx_send[i] = z_sum(1, other, i).astype(BF16)
+    n_zx = send(zx_send, zx_recv, x_mate)
+
     row_lane = lax.broadcasted_iota(jnp.int32, (ND, BS), 1)
-    for i in range(OWN):
-        value = mine[0, i] + x_recv[i].astype(F32)
+
+    def finish(i, value):
         live = row_lane < block_sizes[aux * OWN + i]
         coulomb[i] = jnp.where(live, value, 0.0).astype(BF16)
+
+    for i in range(ZS):
+        z_mine[0, i] = z_sum(0, lo, i)
+    arrived(n_xs3, xs_recv.at[3])
+    arrived(n_xnb0, xnb_recv.at[0])
+    arrived(n_xnb1, xnb_recv.at[1])
+    for i in range(XS):
+        finish(i, x_mine[i] + xs_recv[3, i].astype(F32) + xnb_recv[0, i].astype(F32)
+               + xnb_recv[1, i].astype(F32))
+    arrived(n_zx, zx_recv)
+    for i in range(ZS):
+        finish(XS + i, z_mine[0, i] + zx_recv[i].astype(F32))
 
     for copy in sent:
         copy.wait_send()
@@ -451,8 +490,8 @@
             pltpu.VMEM((ROWS, AUX), BF16),
             pltpu.VMEM((2048, 16, BS), BF16),
             pltpu.VMEM((ND, ROWS), BF16),
-            pltpu.VMEM((ND, HALF), F32),
-            pltpu.VMEM((2, ND, HALF), F32),
+            pltpu.VMEM((2, ND, 256), F32),
+            pltpu.VMEM((2, 2, ND, 256), F32),
             pltpu.VMEM((8, 8, HALF), F32),
             pltpu.VMEM((8, 8, HALF), F32),
             pltpu.VMEM((1280, 3 * HB), F32),
@@ -465,13 +504,20 @@
             pltpu.VMEM((2, 8, HALF), F32),
             pltpu.VMEM((2, 8, 8, HALF), F32),
             pltpu.VMEM((ND, AUX), BF16),
-            pltpu.VMEM((2, OWN, ND, BS), BF16),
-            pltpu.VMEM((2, OWN, ND, BS), BF16),
-            pltpu.VMEM((4, OWN, ND, BS), BF16),
-            pltpu.VMEM((4, OWN, ND, BS), BF16),
-            pltpu.VMEM((OWN, ND, BS), BF16),
-            pltpu.VMEM((OWN, ND, BS), BF16),
-            pltpu.VMEM((2, OWN, ND, BS), F32),
+            pltpu.VMEM((2, ZS, ND, BS), BF16),
+            pltpu.VMEM((2, ZS, ND, BS), BF16),
+            pltpu.VMEM((4, ZS, ND, BS), BF16),
+            pltpu.VMEM((4, ZS, ND, BS), BF16),
+            pltpu.VMEM((ZS, ND, BS), BF16),
+            pltpu.VMEM((ZS, ND, BS), BF16),
+            pltpu.VMEM((2, ZS, ND, BS), F32),
+            pltpu.VMEM((4, XS, ND, BS), BF16),
+            pltpu.VMEM((4, XS, ND, BS), BF16),
+            pltpu.VMEM((XS, ND, BS), BF16),
+            pltpu.VMEM((XS, ND, BS), BF16),
+            pltpu.VMEM((2, XS, ND, BS), BF16),
+            pltpu.VMEM((2, XS, ND, BS), BF16),
+            pltpu.VMEM((XS, ND, BS), F32),
             pltpu.SMEM((4 * SLOTS,), jnp.int32),
             pltpu.SemaphoreType.DMA((NCHUNK,)),
             pltpu.SemaphoreType.DMA((4,)),

time: 100 us -> 77.9 us (0.78)
  Pallas kernels: 95.4 us -> 73.8 us
    pallas_call x1, Pallas kernels: 95.4 us -> 73.8 us  [shards(): pl.pallas_call(kernel, out_shape=(jax.ShapeDtypeStruct((OWN, ND, BS), BF1...]
where the time goes in v2:
time: 77.9 us; the launch traced here: 77.7 us
  Pallas kernels  73.8 us (95%)
  local copies, waits for them, and re-layouts  3.28 us (4%)
    pallas_call x1, Pallas kernels, shards(): pl.pallas_call(kernel, out_shape=(jax.ShapeDtypeStruct((OWN, ND, BS), BF1...  73.8 us
    unnamed x2, local copies, waits for them, and re-layouts  3.28 us

profile of v2, /device:TPU:0, one launch (start us, length us, event | category | flops | bytes accessed | tf_op | source)
XLA Modules:
  0.0 77.7 jit_solution(556110384751285025)
XLA Ops:
  0.6 73.8 %shard_map.68 = (bf16[11,64,128]{2,1,0:T(8,128)(2,1)}, f32[64,1024]{1,0:T(8,128)}) custom-call(s32[88]{0:T(128)} %block_list.1, s32[88]{0:T(128)} %block_sizes.1, bf16[16,16,128]{2,1,0:T(8,128)(2,1)} %bitcast.1, bf16[11264,1024]{1,0:T(8,128)(2,1)} %slab.1, f32[1024,384]{1,0:T(8,128)} %metric.1), custom_call_target="tpu_custom_call" | custom-call | flops 2952790016 | bytes 23068672 | tf_op jit(solution)/shard_map/pallas_call | solution.py:481
  74.5 1.6 %copy.9 = bf16[11,64,128]{2,1,0:T(8,128)(2,1)} copy(bf16[11,64,128]{2,1,0:T(8,128)(2,1)} %get-tuple-element.4) | data formatting | bytes 360448
  76.1 1.7 %copy.10 = f32[64,1024]{1,0:T(8,128)} copy(f32[64,1024]{1,0:T(8,128)} %get-tuple-element.5) | data formatting | bytes 524288

commit v3 on v2

--- a/solution.py
+++ b/solution.py
@@ -21,9 +21,9 @@
 NCHUNK = ROWS // CHUNK
 
 PARTS = (
-    (0, 6, 0, (0, 1, 2)),
-    (6, 5, 768, (1, 2, 0)),
-    (11, 5, 1408, (2, 0, 1)),
+    (0, 5, 0, (0, 1, 2)),
+    (5, 5, 640, (1, 2, 0)),
+    (10, 6, 1280, (2, 0, 1)),
 )
 
 
@@ -33,7 +33,7 @@
 
 def kernel(block_list, block_sizes, density, slab, metric, coulomb, coeffs, *scratch):
     (slab_v, held, picked, acc, sib_acc, fit_send, fit_recv, mw, wh, wl, u0, u, lh,
-     own_u, halo, call, cb, zfar_send, zfar_recv, znb_send, znb_recv, zx_send, zx_recv, z_mine,
+     own_u, halo, call, rounded, cb, z_wait, zfar_send, zfar_recv, znb_send, znb_recv, zx_send, zx_recv, z_mine,
      xs_send, xs_recv, xfar_send, xfar_recv, xnb_send, xnb_recv, x_mine, index, slab_sem, local_sem, send_sem, recv_sem) = scratch
 
     pair = lax.axis_index("pair")
@@ -61,12 +61,16 @@
     sibling = device([x, y, z], 1 - core)
     ext_aux = mod(aux + 2 * core - 1, 8)
     ext = (chip * 2 + (1 - core), ext_aux)
-    chips = [(mod(chip + o, 8) * 2 + core, aux) for o in range(1, 8)]
+    steps = ((1, 2), (1, 1), (1, 3), (1, 0), (0, 2), (0, 1), (0, 3))
+    chip_to = [mod(chip // 4 + flip, 2) * 4 + mod(y + by, 4) for flip, by in steps]
+    chip_from = [mod(chip // 4 + flip, 2) * 4 + mod(y - by, 4) for flip, by in steps]
+    chips = [(to * 2 + core, aux) for to in chip_to]
+    other_cores = [(to * 2 + 1 - core, aux) for to in chip_to]
     x_mate = (pair, mod(aux + 4, 8))
 
     barrier = pltpu.get_barrier_semaphore()
-    partners = [moves[0, 1], moves[0, -1], moves[2, 1], moves[2, -1], moves[2, 2], sibling, ext]
-    partners += chips + [(mod(chip + o, 8) * 2 + 1 - core, aux) for o in range(1, 8)]
+    partners = chips + other_cores
+    partners += [ext, moves[2, 2], moves[0, 1], moves[0, -1], moves[2, 1], moves[2, -1], sibling]
     for partner in partners:
         pl.semaphore_signal(barrier, inc=1, device_id=partner, device_id_type=pl.DeviceIdType.MESH)
 
@@ -82,21 +86,15 @@
     )
     own_metric.start()
 
-    def place(part, i3, i2, i1, at_core):
+    def place(part, far3=0, far2=0, far1=0):
         _, tiles, base, _ = PARTS[part]
-        return base + (((at_core * 4 + i3) * 4 + i2) * 4 + i1) * tiles
-
-    def spot(part):
-        order = PARTS[part][3]
-        coords = (x, y, z)
-        return coords[order[0]], coords[order[1]], coords[order[2]]
+        return base + core * (64 * tiles) + ((far3 * 4 + far2) * 4 + far1) * tiles
 
     own_tiles = []
     for part, (first, tiles, _, _) in enumerate(PARTS):
-        i1, i2, i3 = spot(part)
         copy = pltpu.make_async_copy(
             density.at[pl.ds(first, tiles)],
-            held.at[pl.ds(place(part, i3, i2, i1, core), tiles)],
+            held.at[pl.ds(place(part), tiles)],
             local_sem.at[1 + part],
         )
         copy.start()
@@ -139,63 +137,67 @@
         sib_waits.append((n, window(other, size)))
 
     class Ring:
-        def __init__(self, part, level, start_of, size, cut=0):
-            self.part, self.start_of, self.size, self.cut = part, start_of, size, cut
+        def __init__(self, part, level, first, tiles, cut=0):
+            self.part, self.first, self.size = part, first, tiles
+            self.cut = cut
             self.dim = PARTS[part][3][level]
-            self.at = (x, y, z)[self.dim]
-
-        def piece(self, by):
-            return self.start_of(mod(self.at + by, 4))
-
-        def start(self, src=None):
-            ref = window(self.piece(0), self.size)
-            src = ref if src is None else src
-            self.up = send(src, ref, moved(self.dim, 1))
-            self.down = send(src, ref, moved(self.dim, -1))
+            self.stride = PARTS[part][1] * 4 ** level
+
+        def piece(self, far, start=0, size=None):
+            return window(self.first + far * self.stride + start, self.size if size is None else size)
+
+        def start(self):
+            self.up = send(self.piece(0), self.piece(3), moved(self.dim, 1))
+            self.down = send(self.piece(0), self.piece(1), moved(self.dim, -1))
             if self.cut == 0:
-                self.far = send(src, ref, moved(self.dim, 2))
+                self.far = send(self.piece(0), self.piece(2), moved(self.dim, 2))
 
         def middle(self):
-            arrived(self.up, window(self.piece(-1), self.size))
-            if self.cut == 0:
-                arrived(self.down, window(self.piece(1), self.size))
-                return
-            low = window(self.piece(-1), self.cut)
-            self.up_far = send(low, low, moved(self.dim, 1))
-            arrived(self.down, window(self.piece(1), self.size))
-            high = window(self.piece(1) + self.cut, self.size - self.cut)
-            self.down_far = send(high, high, moved(self.dim, -1))
+            arrived(self.up, self.piece(3))
+            if self.cut:
+                self.up_far = send(self.piece(3, 0, self.cut), self.piece(2, 0, self.cut), moved(self.dim, 1))
+            arrived(self.down, self.piece(1))
+            if self.cut:
+                rest = self.size - self.cut
+                self.down_far = send(self.piece(1, self.cut, rest), self.piece(2, self.cut, rest),
+                                     moved(self.dim, -1))
 
         def end(self):
             if self.cut == 0:
-                arrived(self.far, window(self.piece(2), self.size))
+                arrived(self.far, self.piece(2))
                 return
-            arrived(self.up_far, window(self.piece(2), self.cut))
-            arrived(self.down_far, window(self.piece(2) + self.cut, self.size - self.cut))
-
-        def share(self, *bys):
-            for by in bys:
-                to_sibling(self.part, self.piece(by), self.size)
-
-    first_rings, second_rings, third_rings = [], [], []
-    for part in range(3):
-        first, tiles, _, _ = PARTS[part]
-        i1, i2, i3 = spot(part)
-        first_rings.append(Ring(part, 0, lambda i, part=part, i2=i2, i3=i3: place(part, i3, i2, i, core),
-                                tiles))
-        second_rings.append(Ring(part, 1, lambda i, part=part, i3=i3: place(part, i3, i, 0, core),
-                                 4 * tiles))
-        third_rings.append({
-            by: Ring(part, 2, lambda i, part=part, i2=i2, by=by: place(part, i, mod(i2 + by, 4), 0, core),
-                     4 * tiles, 2 * tiles)
-            for by in (0, -1, 1, 2)
-        })
-
-    for part, ring in enumerate(first_rings):
-        first, tiles, _, _ = PARTS[part]
+            arrived(self.up_far, self.piece(2, 0, self.cut))
+            arrived(self.down_far, self.piece(2, self.cut, self.size - self.cut))
+
+    def every(make):
+        return [make(part, PARTS[part][1]) for part in range(3)]
+
+    first_rings = every(lambda part, t: Ring(part, 0, place(part), t))
+    second_own = every(lambda part, t: Ring(part, 1, place(part), t))
+    second_rest = every(lambda part, t: Ring(part, 1, place(part) + t, 3 * t))
+    third_own = every(lambda part, t: Ring(part, 2, place(part), t, t // 2))
+    third_rest = every(lambda part, t: Ring(part, 2, place(part) + t, 3 * t, 3 * t // 2))
+    third_rows = [None] + [
+        every(lambda part, t, far=far: Ring(part, 2, place(part, 0, far), 4 * t, 2 * t)) for far in (1, 2, 3)
+    ]
+
+    def share(far3, far2, rows=1):
+        for part in range(3):
+            to_sibling(part, place(part, far3, far2), 4 * rows * PARTS[part][1])
+
+    for ring in first_rings + second_own + third_own:
         ring.start()
     for copy in slab_copies:
         copy.start()
+
+    def send_metric(start, rows):
+        src = pl.multiple_of(core * 640 + start, 128)
+        dst = pl.multiple_of(896 - core * 896 + start, 128)
+        here = pl.multiple_of(core * 896 + start, 128)
+        n = send(metric.at[pl.ds(src, rows), :], mw.at[pl.ds(dst, rows), :], ext)
+        return n, mw.at[pl.ds(here, rows), :]
+
+    metric_waits = [send_metric(0, 128)]
 
     def find(s, _):
         b = block_list[s]
@@ -205,39 +207,37 @@
         bc = (b >> 5) & 1
         by = (b >> 6) & 3
         bx = ((b >> 8) & 1) * 2 + blo
+        bx, by, bz = (bx - x) & 3, (by - y) & 3, (bz - z) & 3
         places = (
-            (((bc * 4 + bz) * 4 + by) * 4 + bx) * 6,
-            768 + (((bc * 4 + bx) * 4 + bz) * 4 + by) * 5 - 6,
-            1408 + (((bc * 4 + by) * 4 + bx) * 4 + bz) * 5 - 11,
+            (((bc * 4 + bz) * 4 + by) * 4 + bx) * 5,
+            640 + (((bc * 4 + bx) * 4 + bz) * 4 + by) * 5 - 5,
+            1280 + (((bc * 4 + by) * 4 + bx) * 4 + bz) * 6 - 10,
         )
         for r in range(4):
             t = j * 4 + r
-            index[s * 4 + r] = t + jnp.where(t < 6, places[0], jnp.where(t < 11, places[1], places[2]))
+            index[s * 4 + r] = t + jnp.where(t < 5, places[0], jnp.where(t < 10, places[1], places[2]))
         return 0
 
     for ring in first_rings:
         ring.middle()
     for ring in first_rings:
         ring.end()
-    for part in range(3):
-        second_rings[part].start()
-    for part in range(3):
-        third_rings[part][0].start()
-    for part in range(3):
-        second_rings[part].share(0)
-    for part in range(3):
-        second_rings[part].middle()
-    for part in range(3):
-        third_rings[part][-1].start()
-        third_rings[part][1].start()
-    for part in range(3):
-        second_rings[part].share(-1, 1)
-    for part in range(3):
-        second_rings[part].end()
-    for part in range(3):
-        third_rings[part][2].start()
-    for part in range(3):
-        second_rings[part].share(2)
+    for ring in second_rest + third_rest:
+        ring.start()
+    share(0, 0)
+    for ring in third_own + second_own:
+        ring.middle()
+    for ring in second_rest:
+        ring.middle()
+    for ring in third_rows[3] + third_rows[1]:
+        ring.start()
+    share(0, 3)
+    share(0, 1)
+    for ring in second_own + second_rest:
+        ring.end()
+    for ring in third_rows[2]:
+        ring.start()
+    share(0, 2)
     lax.fori_loop(0, SLOTS, find, 0)
     eye = (lax.broadcasted_iota(jnp.int32, (HB, HB), 0) == lax.broadcasted_iota(jnp.int32, (HB, HB), 1))
     low_ok = jnp.logical_or(aux > 0, core == 1)
@@ -268,11 +268,16 @@
         return 0
 
 
-    for by in (0, -1, 1, 2):
-        for part in range(3):
-            third_rings[part][by].middle()
-        for part in range(3):
-            third_rings[part][by].share(-1, 1)
+    for ring in third_rest:
+        ring.middle()
+    share(3, 0)
+    share(1, 0)
+    for far in (3, 1, 2):
+        for ring in third_rows[far]:
+            ring.middle()
+        share(3, far)
+        share(1, far)
+    metric_waits.append(send_metric(128, 256))
     own_metric.wait()
     lax.fori_loop(0, 3, lambda i, _: build(2 - 2 * core + i), 0)
     diag_rows = []
@@ -280,17 +285,13 @@
         middle = mw[n * HB:(n + 1) * HB, HB:2 * HB]
         diag_rows.append(jnp.sum(jnp.where(eye, middle, 0.0), axis=0, keepdims=True))
     diag_row = jnp.concatenate(diag_rows, axis=1)
-    for by in (0, -1, 1, 2):
-        for part in range(3):
-            third_rings[part][by].end()
-        for part in range(3):
-            third_rings[part][by].share(2)
-    metric_n = send(
-        metric.at[pl.ds(pl.multiple_of(core * 640, 128), 384), :],
-        mw.at[pl.ds(pl.multiple_of(896 - core * 896, 128), 384), :],
-        ext,
-    )
-
+    for ring in third_own + third_rest:
+        ring.end()
+    share(2, 0)
+    for far in (3, 1, 2):
+        for ring in third_rows[far]:
+            ring.end()
+        share(2, far)
     for n, ref in sib_waits:
         arrived(n, ref)
 
@@ -325,16 +326,16 @@
             rows = slice(q * 8, (q + 1) * 8)
             fit_send[q, :, n * 256:(n + 1) * 256] = acc[n, rows, :] + sib_acc[1, n, rows, :]
     waits = []
-    for o in range(1, 8):
-        to = mod(chip + o, 8)
-        n = send(fit_send.at[to], fit_recv.at[o], chips[o - 1])
+    for o, to in enumerate(chip_to):
+        n = send(fit_send.at[to], fit_recv.at[o], chips[o])
         waits.append((n, fit_recv.at[o]))
-    arrived(metric_n, mw.at[pl.ds(pl.multiple_of(core * 896, 128), 384), :])
+    for n, ref in metric_waits:
+        arrived(n, ref)
     lax.fori_loop(0, 2, lambda i, _: build(3 * core + i), 0)
     total = fit_send[chip]
     for o, (n, ref) in enumerate(waits):
         arrived(n, ref)
-        total = total + fit_recv[o + 1]
+        total = total + fit_recv[o]
 
     own_u[...] = total / diag_row
     n_sib = send(own_u, halo.at[core], sibling)
@@ -357,21 +358,26 @@
             cols = slice((2 * i + 1) * HB, (2 * i + 3) * HB)
             u[:, cols] = u0[:, cols] + (one[0:8] + (one[8:16] + two[0:8]))
 
-    call[core, chip] = u[:, HALF:2 * HALF]
-    own_ref = call.at[core, chip]
+    own = u[:, HALF:2 * HALF]
+    call[core, chip] = own
+    rounded[core, chip] = jnp.concatenate([own[:, :256], own[:, 256:]], axis=0).astype(BF16)
+    ref = rounded.at[core, chip]
     waits = []
-    for o in range(1, 8):
-        other = (mod(chip + o, 8) * 2 + 1 - core, aux)
-        waits.append((send(own_ref, own_ref, chips[o - 1]), call.at[core, mod(chip - o, 8)]))
-        waits.append((send(own_ref, own_ref, other), call.at[1 - core, mod(chip - o, 8)]))
-    waits.append((send(own_ref, own_ref, sibling), call.at[1 - core, chip]))
+    for o, source in enumerate(chip_from):
+        waits.append((send(ref, ref, chips[o]), rounded.at[core, source]))
+        waits.append((send(ref, ref, other_cores[o]), rounded.at[1 - core, source]))
+    waits.append((send(ref, ref, sibling), rounded.at[1 - core, chip]))
+    ref = call.at[core, chip]
+    full_waits = [(send(ref, ref, chips[o]), call.at[core, source]) for o, source in enumerate(chip_from)]
     for n, ref in waits:
         arrived(n, ref)
     for half in range(2):
         for q in range(4):
-            value = jnp.concatenate([call[half, 2 * q], call[half, 2 * q + 1]], axis=0)
-            coeffs[q * 16:(q + 1) * 16, half * HALF:(half + 1) * HALF] = value
-            cb[q * 16:(q + 1) * 16, half * HALF:(half + 1) * HALF] = value.astype(BF16)
+            two = [rounded[half, 2 * q + k].astype(F32) for k in range(2)]
+            for k in range(2):
+                part = slice(k * 8, (k + 1) * 8)
+                cb[q * 16:(q + 1) * 16, half * HALF + k * 256:half * HALF + (k + 1) * 256] = (
+                    jnp.concatenate([two[0][part], two[1][part]], axis=0).astype(BF16))
 
     def dots(to, start, slots):
         rows = pl.ds(pl.multiple_of(to * (OWN * BS) + start * BS, BS), slots * BS)
@@ -398,10 +404,15 @@
     lo = aux // 4
     other = 1 - lo
 
+    thirds = (pl.ds(0, 3), pl.ds(3, ZS - 3))
+
+    def send_two(src, dst, to):
+        return [(send(src.at[part], dst.at[part], to), dst.at[part]) for part in thirds]
+
     put(zfar_send.at[0], z_part(z_far))
-    n_zfar0 = send(zfar_send.at[0], zfar_recv.at[0], up)
+    w_zfar0 = send_two(zfar_send.at[0], zfar_recv.at[0], up)
     put(zfar_send.at[1], z_part(4 + z_far))
-    n_zfar1 = send(zfar_send.at[1], zfar_recv.at[1], down)
+    w_zfar1 = send_two(zfar_send.at[1], zfar_recv.at[1], down)
     put(xs_send.at[0], x_part(other * 4 + z_far))
     n_xs0 = send(xs_send.at[0], xs_recv.at[0], x_mate)
     put(znb_send.at[0], z_part(4 + z_up))
@@ -410,23 +421,32 @@
     n_znb1 = send(znb_send.at[1], znb_recv.at[1], down)
     put(xs_send.at[1], x_part(other * 4 + z_up))
     n_xs1 = send(xs_send.at[1], xs_recv.at[1], x_mate)
+    put(z_wait.at[0], z_part(z_up))
+    put(z_wait.at[1], z_part(4 + z_down))
     put(xs_send.at[2], x_part(other * 4 + z_down))
     n_xs2 = send(xs_send.at[2], xs_recv.at[2], x_mate)
 
+    w_znb = [], []
+    for part in range(2):
+        for k, (w_far, to) in enumerate(((w_zfar0, up), (w_zfar1, down))):
+            arrived(*w_far[part])
+            for i in range(3 * part, 3 * part + 3):
+                znb_send[2 + k, i] = (z_wait[k, i] + zfar_recv[k, i].astype(F32)).astype(BF16)
+            ref = znb_recv.at[2 + k].at[thirds[part]]
+            w_znb[part].append((send(znb_send.at[2 + k].at[thirds[part]], ref, to), ref))
+    put(xs_send.at[3], x_part(other * 4 + z))
+    n_xs3 = send(xs_send.at[3], xs_recv.at[3], x_mate)
+    first, second = pl.ds(0, 2), pl.ds(2, XS - 2)
     arrived(n_xs0, xs_recv.at[0])
     put(xfar_send, x_part(lo * 4 + z_far), (xs_recv.at[0], 0))
-    first, second = pl.ds(0, 2), pl.ds(2, XS - 2)
     n_xfar0 = send(xfar_send.at[first], xfar_recv.at[first], up)
     n_xfar1 = send(xfar_send.at[second], xfar_recv.at[second], down)
-    arrived(n_zfar0, zfar_recv.at[0])
-    put(znb_send.at[2], z_part(z_up), (zfar_recv.at[0], 0))
-    n_znb2 = send(znb_send.at[2], znb_recv.at[2], up)
-    arrived(n_zfar1, zfar_recv.at[1])
-    put(znb_send.at[3], z_part(4 + z_down), (zfar_recv.at[1], 0))
-    n_znb3 = send(znb_send.at[3], znb_recv.at[3], down)
-    put(xs_send.at[3], x_part(other * 4 + z))
-    n_xs3 = send(xs_send.at[3], xs_recv.at[3], x_mate)
+    for n, ref in full_waits:
+        arrived(n, ref)
+    n_call = send(call.at[core], call.at[core], sibling)
     put(z_mine.at[1], z_part(other * 4 + z))
+    put(z_mine.at[0], z_part(lo * 4 + z))
+    put(x_mine, x_part(lo * 4 + z))
     arrived(n_xs1, xs_recv.at[1])
     arrived(n_xfar0, xfar_recv.at[first])
     put(xnb_send.at[0], x_part(lo * 4 + z_up), (xs_recv.at[1], 0), (xfar_recv.at[first], 0))
@@ -435,20 +455,27 @@
     arrived(n_xfar1, xfar_recv.at[second])
     put(xnb_send.at[1], x_part(lo * 4 + z_down), (xs_recv.at[2], 0), (xfar_recv.at[second], 2))
     n_xnb1 = send(xnb_send.at[1], xnb_recv.at[1], down)
-    put(z_mine.at[0], z_part(lo * 4 + z))
-    put(x_mine, x_part(lo * 4 + z))
-
-    for k, n in enumerate((n_znb0, n_znb1, n_znb2, n_znb3)):
-        arrived(n, znb_recv.at[k])
+
+    arrived(n_znb0, znb_recv.at[0])
+    arrived(n_znb1, znb_recv.at[1])
 
     def z_sum(k, which, i):
         return (z_mine[k, i] + znb_recv[2 - 2 * which, i].astype(F32)
                 + znb_recv[1 + 2 * which, i].astype(F32))
 
-    for i in range(ZS):
-        zx_send[i] = z_sum(1, other, i).astype(BF16)
-    n_zx = send(zx_send, zx_recv, x_mate)
-
+    w_zx = []
+    for part in range(2):
+        for wait in w_znb[part]:
+            arrived(*wait)
+        for i in range(3 * part, 3 * part + 3):
+            zx_send[i] = z_sum(1, other, i).astype(BF16)
+        ref = zx_recv.at[thirds[part]]
+        w_zx.append((send(zx_send.at[thirds[part]], ref, x_mate), ref))
+
+    arrived(n_call, call.at[1 - core])
+    for half in range(2):
+        for q in range(8):
+            coeffs[q * 8:(q + 1) * 8, half * HALF:(half + 1) * HALF] = call[half, q]
     row_lane = lax.broadcasted_iota(jnp.int32, (ND, BS), 1)
 
     def finish(i, value):
@@ -463,7 +490,8 @@
     for i in range(XS):
         finish(i, x_mine[i] + xs_recv[3, i].astype(F32) + xnb_recv[0, i].astype(F32)
                + xnb_recv[1, i].astype(F32))
-    arrived(n_zx, zx_recv)
+    for wait in w_zx:
+        arrived(*wait)
     for i in range(ZS):
         finish(XS + i, z_mine[0, i] + zx_recv[i].astype(F32))
 
@@ -471,7 +499,12 @@
         copy.wait_send()
 
 
-NSEMS = 180
+NSEMS = 240
+
+
+def deliver(coulomb, coeffs, coulomb_out, coeffs_out):
+    coulomb_out[...] = coulomb[...]
+    coeffs_out[...] = coeffs[...]
 
 
 def shards(slab, density, block_list, block_sizes, metric):
@@ -493,7 +526,7 @@
             pltpu.VMEM((2, ND, 256), F32),
             pltpu.VMEM((2, 2, ND, 256), F32),
             pltpu.VMEM((8, 8, HALF), F32),
-            pltpu.VMEM((8, 8, HALF), F32),
+            pltpu.VMEM((7, 8, HALF), F32),
             pltpu.VMEM((1280, 3 * HB), F32),
             pltpu.VMEM((5, 512, 256), BF16),
             pltpu.VMEM((5, 512, 256), BF16),
@@ -503,7 +536,9 @@
             pltpu.VMEM((8, HALF), F32),
             pltpu.VMEM((2, 8, HALF), F32),
             pltpu.VMEM((2, 8, 8, HALF), F32),
+            pltpu.VMEM((2, 8, 16, 256), BF16),
             pltpu.VMEM((ND, AUX), BF16),
+            pltpu.VMEM((2, ZS, ND, BS), F32),
             pltpu.VMEM((2, ZS, ND, BS), BF16),
             pltpu.VMEM((2, ZS, ND, BS), BF16),
             pltpu.VMEM((4, ZS, ND, BS), BF16),
@@ -529,7 +564,15 @@
         ),
         cost_estimate=pl.CostEstimate(flops=4 * ND * ROWS * AUX, bytes_accessed=2 * ROWS * AUX, transcendentals=0),
     )(block_list, block_sizes, density.reshape(16, 16, BS), slab, metric)
-    return coulomb, coeffs
+    return pl.pallas_call(
+        deliver,
+        out_shape=(
+            jax.ShapeDtypeStruct(coulomb.shape, coulomb.dtype),
+            jax.ShapeDtypeStruct(coeffs.shape, coeffs.dtype),
+        ),
+        in_specs=[vmem, vmem],
+        out_specs=(vmem, vmem),
+    )(coulomb, coeffs)
 
 
 def solution(mesh):

time: 77.9 us -> 75.1 us (0.964)
  local copies, waits for them, and re-layouts: 3.28 us -> 0 us
    unnamed x2 -> x0, local copies, waits for them, and re-layouts: 3.28 us -> none
    pallas_call x0 -> x1, Pallas kernels: none -> 1.82 us  [shards(): pl.pallas_call(deliver, out_shape=(jax.ShapeDtypeStruct(coulomb.shape, co...]
    pallas_call x1, Pallas kernels: 73.8 us -> 72 us  [shards(): pl.pallas_call(kernel, out_shape=(jax.ShapeDtypeStruct((OWN, ND, BS), BF1...]
where the time goes in v3:
time: 75.1 us; the launch traced here: 74.5 us
  Pallas kernels  73.8 us (98%)
    pallas_call x1, Pallas kernels, shards(): pl.pallas_call(kernel, out_shape=(jax.ShapeDtypeStruct((OWN, ND, BS), BF1...  72 us
    pallas_call x1, Pallas kernels, shards(): pl.pallas_call(deliver, out_shape=(jax.ShapeDtypeStruct(coulomb.shape, co...  1.82 us

profile of v3, /device:TPU:0, one launch (start us, length us, event | category | flops | bytes accessed | tf_op | source)
XLA Modules:
  0.0 74.5 jit_solution(11557588262349656236)
XLA Ops:
  0.6 72.0 %shard_map.68 = (bf16[11,64,128]{2,1,0:T(8,128)(2,1)}, f32[64,1024]{1,0:T(8,128)}) custom-call(s32[88]{0:T(128)} %block_list.1, s32[88]{0:T(128)} %block_sizes.1, bf16[16,16,128]{2,1,0:T(8,128)(2,1)} %bitcast.1, bf16[11264,1024]{1,0:T(8,128)(2,1)} %slab.1, f32[1024,384]{1,0:T(8,128)} %metric.1), custom_call_target="tpu_custom_call" | custom-call | flops 2952790016 | bytes 23068672 | tf_op jit(solution)/shard_map/pallas_call | solution.py:514
  72.7 1.8 %shard_map.69 = (bf16[11,64,128]{2,1,0:T(8,128)(2,1)}, f32[64,1024]{1,0:T(8,128)}) custom-call(bf16[11,64,128]{2,1,0:T(8,128)(2,1)} %get-tuple-element.4.coulomb, f32[64,1024]{1,0:T(8,128)} %get-tuple-element.5.coeffs), custom_call_target="tpu_custom_call" | custom-call | tf_op jit(solution)/shard_map/pallas_call | solution.py:567

commit v4 on v3

--- a/solution.py
+++ b/solution.py
@@ -33,7 +33,7 @@
 
 def kernel(block_list, block_sizes, density, slab, metric, coulomb, coeffs, *scratch):
     (slab_v, held, picked, acc, sib_acc, fit_send, fit_recv, mw, wh, wl, u0, u, lh,
-     own_u, halo, call, rounded, cb, z_wait, zfar_send, zfar_recv, znb_send, znb_recv, zx_send, zx_recv, z_mine,
+     own_u, halo, call, rounded, cb, z_wait, x_wait, zfar_send, zfar_recv, znb_send, znb_recv, zx_send, zx_recv, z_mine,
      xs_send, xs_recv, xfar_send, xfar_recv, xnb_send, xnb_recv, x_mine, index, slab_sem, local_sem, send_sem, recv_sem) = scratch
 
     pair = lax.axis_index("pair")
@@ -218,6 +218,7 @@
             index[s * 4 + r] = t + jnp.where(t < 5, places[0], jnp.where(t < 10, places[1], places[2]))
         return 0
 
+    lax.fori_loop(0, SLOTS // 2, find, 0)
     for ring in first_rings:
         ring.middle()
     for ring in first_rings:
@@ -227,6 +228,7 @@
     share(0, 0)
     for ring in third_own + second_own:
         ring.middle()
+    lax.fori_loop(SLOTS // 2, SLOTS, find, 0)
     for ring in second_rest:
         ring.middle()
     for ring in third_rows[3] + third_rows[1]:
@@ -238,7 +240,6 @@
     for ring in third_rows[2]:
         ring.start()
     share(0, 2)
-    lax.fori_loop(0, SLOTS, find, 0)
     eye = (lax.broadcasted_iota(jnp.int32, (HB, HB), 0) == lax.broadcasted_iota(jnp.int32, (HB, HB), 1))
     low_ok = jnp.logical_or(aux > 0, core == 1)
     high_ok = jnp.logical_or(aux < 7, core == 0)
@@ -304,7 +305,7 @@
             picked[r * 16:(r + 1) * 16, column] = held[index[s * 4 + r]] * live
         return 0
 
-    lax.fori_loop(0, SLOTS, pick, 0)
+    lax.fori_loop(0, SLOTS, pick, 0, unroll=8)
 
     for copy in slab_copies:
         copy.wait()
@@ -315,7 +316,8 @@
             out[n] = jnp.dot(picked[...], slab_v[:, columns], preferred_element_type=F32)
             return 0
 
-        lax.fori_loop(0, 2, step, 0)
+        for n in range(2):
+            step(n, 0)
 
     fit(sib_acc.at[0], 1 - core)
     n = send(sib_acc.at[0], sib_acc.at[1], sibling)
@@ -409,51 +411,62 @@
     def send_two(src, dst, to):
         return [(send(src.at[part], dst.at[part], to), dst.at[part]) for part in thirds]
 
+    def x_out(k, to):
+        put(xs_send.at[k], x_part(other * 4 + to))
+        return send(xs_send.at[k], xs_recv.at[k], x_mate)
+
+    n_xs0 = x_out(0, z_far)
     put(zfar_send.at[0], z_part(z_far))
     w_zfar0 = send_two(zfar_send.at[0], zfar_recv.at[0], up)
     put(zfar_send.at[1], z_part(4 + z_far))
     w_zfar1 = send_two(zfar_send.at[1], zfar_recv.at[1], down)
-    put(xs_send.at[0], x_part(other * 4 + z_far))
-    n_xs0 = send(xs_send.at[0], xs_recv.at[0], x_mate)
+    n_xs1 = x_out(1, z_up)
+    n_xs2 = x_out(2, z_down)
     put(znb_send.at[0], z_part(4 + z_up))
     n_znb0 = send(znb_send.at[0], znb_recv.at[0], up)
     put(znb_send.at[1], z_part(z_down))
     n_znb1 = send(znb_send.at[1], znb_recv.at[1], down)
-    put(xs_send.at[1], x_part(other * 4 + z_up))
-    n_xs1 = send(xs_send.at[1], xs_recv.at[1], x_mate)
     put(z_wait.at[0], z_part(z_up))
     put(z_wait.at[1], z_part(4 + z_down))
-    put(xs_send.at[2], x_part(other * 4 + z_down))
-    n_xs2 = send(xs_send.at[2], xs_recv.at[2], x_mate)
 
     w_znb = [], []
-    for part in range(2):
+
+    def pass_on(part):
         for k, (w_far, to) in enumerate(((w_zfar0, up), (w_zfar1, down))):
             arrived(*w_far[part])
             for i in range(3 * part, 3 * part + 3):
                 znb_send[2 + k, i] = (z_wait[k, i] + zfar_recv[k, i].astype(F32)).astype(BF16)
             ref = znb_recv.at[2 + k].at[thirds[part]]
             w_znb[part].append((send(znb_send.at[2 + k].at[thirds[part]], ref, to), ref))
-    put(xs_send.at[3], x_part(other * 4 + z))
-    n_xs3 = send(xs_send.at[3], xs_recv.at[3], x_mate)
+
+    pass_on(0)
     first, second = pl.ds(0, 2), pl.ds(2, XS - 2)
+    put(x_mine, x_part(lo * 4 + z_far))
     arrived(n_xs0, xs_recv.at[0])
-    put(xfar_send, x_part(lo * 4 + z_far), (xs_recv.at[0], 0))
+    for i in range(XS):
+        xfar_send[i] = (x_mine[i] + xs_recv[0, i].astype(F32)).astype(BF16)
     n_xfar0 = send(xfar_send.at[first], xfar_recv.at[first], up)
     n_xfar1 = send(xfar_send.at[second], xfar_recv.at[second], down)
+    pass_on(1)
+    n_xs3 = x_out(3, z)
+    put(x_wait.at[0], x_part(lo * 4 + z_up))
+    put(x_wait.at[1], x_part(lo * 4 + z_down))
     for n, ref in full_waits:
         arrived(n, ref)
     n_call = send(call.at[core], call.at[core], sibling)
     put(z_mine.at[1], z_part(other * 4 + z))
     put(z_mine.at[0], z_part(lo * 4 + z))
-    put(x_mine, x_part(lo * 4 + z))
     arrived(n_xs1, xs_recv.at[1])
     arrived(n_xfar0, xfar_recv.at[first])
-    put(xnb_send.at[0], x_part(lo * 4 + z_up), (xs_recv.at[1], 0), (xfar_recv.at[first], 0))
+    for i in range(XS):
+        value = x_wait[0, i] + xs_recv[1, i].astype(F32)
+        xnb_send[0, i] = ((value + xfar_recv[i].astype(F32)) if i < 2 else value).astype(BF16)
     n_xnb0 = send(xnb_send.at[0], xnb_recv.at[0], up)
     arrived(n_xs2, xs_recv.at[2])
     arrived(n_xfar1, xfar_recv.at[second])
-    put(xnb_send.at[1], x_part(lo * 4 + z_down), (xs_recv.at[2], 0), (xfar_recv.at[second], 2))
+    for i in range(XS):
+        value = x_wait[1, i] + xs_recv[2, i].astype(F32)
+        xnb_send[1, i] = ((value + xfar_recv[i].astype(F32)) if i >= 2 else value).astype(BF16)
     n_xnb1 = send(xnb_send.at[1], xnb_recv.at[1], down)
 
     arrived(n_znb0, znb_recv.at[0])
@@ -463,6 +476,7 @@
         return (z_mine[k, i] + znb_recv[2 - 2 * which, i].astype(F32)
                 + znb_recv[1 + 2 * which, i].astype(F32))
 
+    put(x_mine, x_part(lo * 4 + z))
     w_zx = []
     for part in range(2):
         for wait in w_znb[part]:
@@ -539,6 +553,7 @@
             pltpu.VMEM((2, 8, 16, 256), BF16),
             pltpu.VMEM((ND, AUX), BF16),
             pltpu.VMEM((2, ZS, ND, BS), F32),
+            pltpu.VMEM((2, XS, ND, BS), F32),
             pltpu.VMEM((2, ZS, ND, BS), BF16),
             pltpu.VMEM((2, ZS, ND, BS), BF16),
             pltpu.VMEM((4, ZS, ND, BS), BF16),

time: 75.1 us -> 74 us (0.985)
  no operation moved by 1% of the time
where the time goes in v4:
time: 74 us; the launch traced here: 73.8 us
  Pallas kernels  73.2 us (99%)
    pallas_call x1, Pallas kernels, shards(): pl.pallas_call(kernel, out_shape=(jax.ShapeDtypeStruct((OWN, ND, BS), BF1...  71.4 us
    pallas_call x1, Pallas kernels, shards(): pl.pallas_call(deliver, out_shape=(jax.ShapeDtypeStruct(coulomb.shape, co...  1.82 us

profile of v4, /device:TPU:0, one launch (start us, length us, event | category | flops | bytes accessed | tf_op | source)
XLA Modules:
  0.0 73.8 jit_solution(17477076185814564913)
XLA Ops:
  0.6 71.4 %shard_map.68 = (bf16[11,64,128]{2,1,0:T(8,128)(2,1)}, f32[64,1024]{1,0:T(8,128)}) custom-call(s32[88]{0:T(128)} %block_list.1, s32[88]{0:T(128)} %block_sizes.1, bf16[16,16,128]{2,1,0:T(8,128)(2,1)} %bitcast.1, bf16[11264,1024]{1,0:T(8,128)(2,1)} %slab.1, f32[1024,384]{1,0:T(8,128)} %metric.1), custom_call_target="tpu_custom_call" | custom-call | flops 2952790016 | bytes 23068672 | tf_op jit(solution)/shard_map/pallas_call | solution.py:528
  72.0 1.8 %shard_map.69 = (bf16[11,64,128]{2,1,0:T(8,128)(2,1)}, f32[64,1024]{1,0:T(8,128)}) custom-call(bf16[11,64,128]{2,1,0:T(8,128)(2,1)} %get-tuple-element.4.coulomb, f32[64,1024]{1,0:T(8,128)} %get-tuple-element.5.coeffs), custom_call_target="tpu_custom_call" | custom-call | tf_op jit(solution)/shard_map/pallas_call | solution.py:582

commit v5 on v4

--- a/solution.py
+++ b/solution.py
@@ -173,8 +173,8 @@
         return [make(part, PARTS[part][1]) for part in range(3)]
 
     first_rings = every(lambda part, t: Ring(part, 0, place(part), t))
-    second_own = every(lambda part, t: Ring(part, 1, place(part), t))
-    second_rest = every(lambda part, t: Ring(part, 1, place(part) + t, 3 * t))
+    second_own = every(lambda part, t: Ring(part, 1, place(part), t, t // 2))
+    second_rest = every(lambda part, t: Ring(part, 1, place(part) + t, 3 * t, 3 * t // 2))
     third_own = every(lambda part, t: Ring(part, 2, place(part), t, t // 2))
     third_rest = every(lambda part, t: Ring(part, 2, place(part) + t, 3 * t, 3 * t // 2))
     third_rows = [None] + [

time: 74 us -> 72.4 us (0.978)
  Pallas kernels: 73.2 us -> 71.6 us
    pallas_call x1, Pallas kernels: 71.4 us -> 69.8 us  [shards(): pl.pallas_call(kernel, out_shape=(jax.ShapeDtypeStruct((OWN, ND, BS), BF1...]
where the time goes in v5:
time: 72.4 us; the launch traced here: 72.2 us
  Pallas kernels  71.6 us (99%)
    pallas_call x1, Pallas kernels, shards(): pl.pallas_call(kernel, out_shape=(jax.ShapeDtypeStruct((OWN, ND, BS), BF1...  69.8 us
    pallas_call x1, Pallas kernels, shards(): pl.pallas_call(deliver, out_shape=(jax.ShapeDtypeStruct(coulomb.shape, co...  1.82 us

profile of v5, /device:TPU:0, one launch (start us, length us, event | category | flops | bytes accessed | tf_op | source)
XLA Modules:
  0.0 72.2 jit_solution(1712113763037237625)
XLA Ops:
  0.6 69.8 %shard_map.68 = (bf16[11,64,128]{2,1,0:T(8,128)(2,1)}, f32[64,1024]{1,0:T(8,128)}) custom-call(s32[88]{0:T(128)} %block_list.1, s32[88]{0:T(128)} %block_sizes.1, bf16[16,16,128]{2,1,0:T(8,128)(2,1)} %bitcast.1, bf16[11264,1024]{1,0:T(8,128)(2,1)} %slab.1, f32[1024,384]{1,0:T(8,128)} %metric.1), custom_call_target="tpu_custom_call" | custom-call | flops 2952790016 | bytes 23068672 | tf_op jit(solution)/shard_map/pallas_call | solution.py:528
  70.4 1.8 %shard_map.69 = (bf16[11,64,128]{2,1,0:T(8,128)(2,1)}, f32[64,1024]{1,0:T(8,128)}) custom-call(bf16[11,64,128]{2,1,0:T(8,128)(2,1)} %get-tuple-element.4.coulomb, f32[64,1024]{1,0:T(8,128)} %get-tuple-element.5.coeffs), custom_call_target="tpu_custom_call" | custom-call | tf_op jit(solution)/shard_map/pallas_call | solution.py:582
